TPU v7x, 256 devices: a whole 4x4x8 slice. The times are simulated.
256 devices in a mesh: section: 2 (over x_hi), expert: 64 (over z, y, x_lo), dp: 2 (over core).
Axes of the slice: x: 4 (x_hi: 2, x_lo: 2; x = x_hi * 2 + x_lo), y: 4, z: 8, core: 2. Of those that a mesh axis runs over, the one named last changes fastest.
Arguments:
- layer_input: bfloat16 [2, 2, 8192, 2048], P('section', 'dp', 'expert'), may hold values from -6 to 6
- grad_output: bfloat16 [2, 2, 8192, 2048], P('section', 'dp', 'expert'), may hold values from -3 to 3
- selections: int32 [2, 2, 16, 512], P('section', 'dp'), may hold values from 0 to 8191, as said below
- gate_values: float32 [2, 2, 16, 512], P('section', 'dp'), may hold values from 0.1 to 1
- gate_weight: bfloat16 [2, 64, 2048, 256], P('section', 'expert', 'dp'), may hold values from -0.125 to 0.125
- up_weight: bfloat16 [2, 64, 2048, 256], P('section', 'expert', 'dp'), may hold values from -0.125 to 0.125
- down_weight: bfloat16 [2, 64, 256, 2048], P('section', 'expert', None, 'dp'), may hold values from -0.1875 to 0.1875
Outputs:
- incoming_grad: bfloat16 [2, 2, 8192, 2048], P('section', 'dp', 'expert')
- gate_grad: float32 [2, 2, 16, 512], P('section', 'dp')
- gate_weight_grad: float32 [2, 64, 2048, 256], P('section', 'expert', 'dp')
- up_weight_grad: float32 [2, 64, 2048, 256], P('section', 'expert', 'dp')
- down_weight_grad: float32 [2, 64, 256, 2048], P('section', 'expert', None, 'dp')
Inputs may be any that keep to these rules, and one draw needn't show every extreme that they name: Row e of selections[s, b] lists 512 distinct tokens of micro-batch b, in no particular order. Of the 128 tokens k * 128 to (k + 1) * 128 - 1, one expert takes at most 16, and every expert takes exactly 16 from some such block.
All inputs are finite; a program needn't handle non-finite values.
Results may differ from a plain program's by a relative error of at most 0.0085.
Values may be sent and summed in bfloat16 or wider, within the bound.
A program may use at most 128 MiB of HBM per device.

v0:
```python
import jax
import jax.numpy as jnp
from jax import lax
from jax.sharding import PartitionSpec as P

SPLIT = 4


def shifted(block, axis, distance):
    devices = range(lax.axis_size(axis))
    route = [(i - distance, i) for i in devices if i - distance in devices]
    return lax.ppermute(block, axis, route)


def contract_rows(left, right):
    return lax.dot_general(
        left, right, (((0,), (0,)), ((), ())), preferred_element_type=jnp.float32
    )


def contract_last(left, right):
    return lax.dot_general(
        left, right, (((1,), (1,)), ((), ())), preferred_element_type=jnp.float32
    )


def on_device(
    layer_input, grad_output, selections, gate_values, gate_weight, up_weight, down_weight
):
    expert_devices = lax.axis_size("expert")
    expert_rank = lax.axis_index("expert")
    token_count = layer_input.shape[2]
    model_width = layer_input.shape[3]
    slot_count = token_count // 8
    total_slots = expert_devices * slot_count
    chosen = selections[0, 0]
    experts_here = chosen.shape[0]
    owner_expert = expert_rank // SPLIT
    source_block = chosen // token_count
    local_index = chosen - source_block * token_count
    block_hits = (
        source_block[:, :, None] == jnp.arange(expert_devices, dtype=jnp.int32)[None, None, :]
    ).astype(jnp.int32)
    earlier = jnp.cumsum(block_hits, axis=1) - block_hits
    slot_index = jnp.sum(earlier * block_hits, axis=2)
    from_here = source_block == expert_rank
    expert_ids = jnp.broadcast_to(jnp.arange(experts_here, dtype=jnp.int32)[:, None], chosen.shape)
    slot_table = jnp.full((experts_here, slot_count + 1), token_count, jnp.int32)
    slot_table = slot_table.at[expert_ids, jnp.where(from_here, slot_index, slot_count)].set(
        jnp.where(from_here, local_index, token_count)
    )
    slot_table = slot_table[:, :slot_count]
    send_table = jnp.repeat(slot_table, SPLIT, axis=0).reshape(-1)
    rows_here = layer_input[0, 0]
    grads_here = grad_output[0, 0]
    own_block = lax.dynamic_index_in_dim(source_block, owner_expert, 0, keepdims=False)
    own_slot = lax.dynamic_index_in_dim(slot_index, owner_expert, 0, keepdims=False)
    flat_slot = own_block * slot_count + own_slot
    gate_rows = lax.dynamic_index_in_dim(gate_values[0, 0], owner_expert, 0, keepdims=False)
    blank_row = jnp.zeros((1, model_width), jnp.bfloat16)
    sent_rows = jnp.concatenate([rows_here, blank_row], axis=0)[slot_table]
    sent_grads = jnp.concatenate([grads_here, blank_row], axis=0)[slot_table]
    sent_rows = jnp.repeat(sent_rows, SPLIT, axis=0)
    sent_grads = jnp.repeat(sent_grads, SPLIT, axis=0)
    got_rows, got_grads = (
        lax.all_to_all(sent_rows, "expert", split_axis=0, concat_axis=0, tiled=True),
        lax.all_to_all(sent_grads, "expert", split_axis=0, concat_axis=0, tiled=True),
    )
    got_rows = got_rows.reshape(total_slots, model_width)
    got_grads = got_grads.reshape(total_slots, model_width)
    rows_in = got_rows[flat_slot]
    rows_grad = got_grads[flat_slot]
    gate_full, up_full, down_full = (
        lax.all_gather(gate_weight, "dp", axis=2, tiled=True),
        lax.all_gather(up_weight, "dp", axis=2, tiled=True),
        lax.all_gather(down_weight, "dp", axis=3, tiled=True),
    )
    gate_full = gate_full[0, 0]
    up_full = up_full[0, 0]
    down_full = down_full[0, 0]
    hidden = gate_full.shape[1]
    batches = lax.axis_size("dp")
    gate_pre = jnp.dot(rows_in, gate_full, preferred_element_type=jnp.float32)
    up_pre = jnp.dot(rows_in, up_full, preferred_element_type=jnp.float32)
    sigmoid_gate = jax.nn.sigmoid(gate_pre)
    swish_gate = gate_pre * sigmoid_gate
    activation = (swish_gate * up_pre).astype(jnp.bfloat16)
    gated_grad = (gate_rows[:, None] * rows_grad.astype(jnp.float32)).astype(jnp.bfloat16)
    upstream = contract_last(rows_grad, down_full)
    gate_part = jnp.sum(activation.astype(jnp.float32) * upstream, axis=1)
    scaled = gate_rows[:, None] * upstream
    grad_gate_pre = (
        scaled * up_pre * sigmoid_gate * (1.0 + gate_pre * (1.0 - sigmoid_gate))
    ).astype(jnp.bfloat16)
    grad_up_pre = (scaled * swish_gate).astype(jnp.bfloat16)
    input_part = (
        contract_last(grad_gate_pre, gate_full) + contract_last(grad_up_pre, up_full)
    ).astype(jnp.bfloat16)
    returning = jnp.zeros((total_slots, model_width), jnp.bfloat16).at[flat_slot].set(input_part)
    returned = lax.all_to_all(
        returning.reshape(expert_devices, slot_count, model_width),
        "expert",
        split_axis=0,
        concat_axis=0,
        tiled=True,
    )
    returned = returned.reshape(total_slots, model_width)
    summed = (
        jnp.zeros((token_count + 1, model_width), jnp.float32)
        .at[send_table]
        .add(returned.astype(jnp.float32))
    )
    summed = summed[:token_count]
    incoming_grad = shifted(summed.astype(jnp.bfloat16)[None, None], "section", -1)
    partial_gates = jnp.where(
        jnp.arange(experts_here, dtype=jnp.int32)[:, None] == owner_expert, gate_part[None, :], 0.0
    )
    gate_grad = lax.psum(partial_gates, "expert")[None, None]
    reduced = lax.psum_scatter(
        jnp.concatenate(
            [
                jnp.concatenate(
                    [contract_rows(rows_in, grad_gate_pre), contract_rows(rows_in, grad_up_pre)],
                    axis=1,
                ),
                contract_rows(gated_grad, activation),
            ],
            axis=1,
        ).astype(jnp.bfloat16),
        "dp",
        scatter_dimension=0,
        tiled=True,
    ).astype(jnp.float32)
    gate_up_sum = reduced[:, : 2 * hidden]
    down_sum = reduced[:, 2 * hidden :]
    gate_weight_grad = (gate_up_sum[:, :hidden] / batches)[None, None]
    up_weight_grad = (gate_up_sum[:, hidden:] / batches)[None, None]
    down_weight_grad = (down_sum.T / batches)[None, None]
    return (incoming_grad, gate_grad, gate_weight_grad, up_weight_grad, down_weight_grad)


def solution(mesh):
    return jax.shard_map(
        on_device,
        mesh=mesh,
        in_specs=(
            P("section", "dp", "expert", None),
            P("section", "dp", "expert", None),
            P("section", "dp", None, None),
            P("section", "dp", None, None),
            P("section", "expert", "dp", None),
            P("section", "expert", "dp", None),
            P("section", "expert", None, "dp"),
        ),
        out_specs=(
            P("section", "dp", "expert", None),
            P("section", "dp", None, None),
            P("section", "expert", "dp", None),
            P("section", "expert", "dp", None),
            P("section", "expert", None, "dp"),
        ),
        check_vma=False,
    )
```

profile of v0, /device:TPU:8, one launch (start us, length us, event | category | flops | bytes accessed | tf_op | source)
XLA Modules:
  0.0 753.4 jit_solution(1655733607561743241)
XLA Ops:
  7.2 0.0 copy-start
  7.2 0.8 squeeze.30
  8.0 0.8 fusion.32
  8.8 1.6 fusion.8
  10.4 34.0 %reduce-window.6 = s32[16,64,4,128]{3,1,2,0:T(8,128)S(1)} reduce-window(s32[16,64,4,128]{3,1,2,0:T(8,128)} %fusion.8, s32[]{:T(128)} %constant.69.clone.1), window={size=1x1x1x128 pad=0_0x0_0x0_0x127_0}, to_apply=%region_0.1 | reduce-window | flops 66584576 | bytes 4194308 | tf_op jit(solution)/shard_map/reduce-window
  44.4 2.0 slice.40
  46.4 2.3 copy.14
  48.7 0.1 fusion.28
  48.9 0.7 fusion.4
  49.6 0.0 copy-done.7
  49.7 0.0 copy-done.9
  49.7 0.1 multiply_reduce_fusion.1
  49.7 0.0 copy-done.8
  49.7 0.1 and_reduce_fusion
  49.9 30.4 %scatter_custom_fusion.2 = s32[272]{0:T(512)S(1)} fusion(s32[8192]{0:T(1024)S(1)} %bitcast.135, s32[8192]{0:T(1024)S(1)} %bitcast.136, s32[]{:T(128)} %constant.40.clone.1), kind=kCustom, calls=%fused_computation.93 | custom fusion | bytes 1092
  80.3 0.1 reshape.238
  80.4 0.1 reshape.242
  80.5 0.0 copy-done.5
  80.6 1.4 gather_fusion
  81.9 2.5 broadcast_in_dim.85
  84.4 13.3 %all-to-all-start = ((bf16[64,16,2048]{2,1,0:T(8,128)(2,1)}), bf16[64,16,2048]{2,1,0:T(8,128)(2,1)}, u32[]{:S(2)}, u32[]{:S(2)}) async-start(bf16[64,16,2048]{2,1,0:T(8,128)(2,1)} %bitcast.129), calls=%async_computation | async-start | bytes 8388608 | tf_op jit(solution)/shard_map/all_to_all | solution.py:67
  97.8 0.0 copy-done.6
  97.9 1.4 gather_fusion.2
  99.2 93.8 %all-to-all-done = bf16[64,16,2048]{2,1,0:T(8,128)(2,1)} async-done(((bf16[64,16,2048]{2,1,0:T(8,128)(2,1)}), bf16[64,16,2048]{2,1,0:T(8,128)(2,1)}, u32[]{:S(2)}, u32[]{:S(2)}) %all-to-all-start) | async-done | bytes 4194336 | tf_op jit(solution)/shard_map/all_to_all | solution.py:67
  193.0 2.5 broadcast_in_dim.86
  195.5 7.0 all-to-all-start.1
  202.5 0.0 all-gather.8.cloned.1.call-start
  202.6 0.7 all-gather.8.cloned.1.call-update
  203.3 0.0 all-gather.6.cloned.1.call-start
  203.3 0.7 all-gather.6.cloned.1.call-update
  204.0 0.0 all-gather.4.cloned.1.call-start
  204.1 0.7 all-gather.4.cloned.1.call-update
  204.9 8.1 %gather_fusion.1 = bf16[512,2048]{1,0:T(8,128)(2,1)} fusion(bf16[1024,2048]{1,0:T(8,128)(2,1)} %bitcast.12, s32[1024]{0:T(1024)S(1)} %pad_clamp_fusion), kind=kCustom, calls=%fused_computation.1 | custom fusion | bytes 4196352 | tf_op jit(solution)/shard_map/gather | solution.py:72
  213.0 83.2 %all-to-all-done.1 = bf16[64,16,2048]{2,1,0:T(8,128)(2,1)} async-done(((bf16[64,16,2048]{2,1,0:T(8,128)(2,1)}), bf16[64,16,2048]{2,1,0:T(8,128)(2,1)}, u32[]{:S(2)}, u32[]{:S(2)}) %all-to-all-start.1) | async-done | bytes 4194336 | tf_op jit(solution)/shard_map/all_to_all | solution.py:66
  296.2 7.1 gather_fusion.3
  303.4 0.0 all-gather.8.cloned.1.call-done
  303.4 2.8 fusion.14
  306.2 2.8 fusion.17
  308.9 3.2 multiply_reduce_fusion
  312.1 0.8 fusion.12
  312.9 0.5 copy-done.4
  313.4 2.1 add_convert_fusion
  315.5 7.4 scatter_custom_fusion
  322.9 7.0 all-to-all-start.2
  329.9 0.0 reduce-scatter.2.cloned.1.call-start
  330.0 0.7 convolution_convert_fusion.2
  330.7 0.7 convolution_convert_fusion.1
  331.4 0.9 copy-done.2
  332.3 0.8 convolution_convert_fusion
  333.1 1.9 pad_maximum_fusion
  335.1 0.0 reduce-scatter.2.cloned.1.call-update
  335.1 0.1 reshape_reshape.3
  335.2 88.4 %all-to-all-done.2 = bf16[64,16,2048]{2,1,0:T(8,128)(2,1)} async-done(((bf16[64,16,2048]{2,1,0:T(8,128)(2,1)}), bf16[64,16,2048]{2,1,0:T(8,128)(2,1)}, u32[]{:S(2)}, u32[]{:S(2)}) %all-to-all-start.2) | async-done | bytes 4194336 | tf_op jit(solution)/shard_map/all_to_all | solution.py:100
  423.6 14.9 %scatter_custom_fusion.1 = f32[129,2048]{1,0:T(8,128)S(1)} fusion(s32[1024]{0:T(1024)S(1)} %bitcast.139, bf16[1024,2048]{1,0:T(8,128)(2,1)} %bitcast.28, f32[]{:T(128)} %constant.39.clone.1), kind=kCustom, calls=%fused_computation.7 | custom fusion | flops 4194304 | bytes 5251076 | tf_op jit(solution)/shard_map/scatter-add | solution.py:111
  438.5 0.1 fusion.22
  438.6 1.3 collective-permute-start
  439.9 0.1 select_bitcast_fusion.1
  440.0 300.4 %psum.7 = f32[1,1,16,512]{3,2,1,0:T(8,128)} all-reduce(f32[1,1,16,512]{3,2,1,0:T(8,128)S(1)} %select_bitcast_fusion.1), channel_id=1, replica_groups=mesh['section'=2,'expert'=64,'dp'=2] {'expert'}, use_global_device_ids=true, to_apply=%region_7.8 | all-reduce | flops 8192 | bytes 65536 | tf_op jit(solution)/shard_map/psum | solution.py:118
  740.4 1.8 convert_element_type.50
  742.2 1.3 fusion.9
  743.5 1.3 copy.17
  744.8 1.3 copy.18
  746.1 0.0 collective-permute-done
  746.1 0.8 copy.24
  (33 shorter events, 0.3 us)
Async XLA Ops:
  7.2 197.7 %copy-start = (f32[1,1,16,512]{3,2,1,0:T(8,128)S(1)}, f32[1,1,16,512]{3,2,1,0:T(8,128)}, u32[]{:S(2)}) copy-start(f32[1,1,16,512]{3,2,1,0:T(8,128)} %param.10) | copy-start | bytes 98308
  46.4 3.2 copy-start.7
  46.4 3.3 copy-start.9
  46.4 3.4 copy-start.8
  46.4 34.1 %copy-start.5 = (bf16[1,1,128,2048]{3,2,1,0:T(8,128)(2,1)S(1)}, bf16[1,1,128,2048]{3,2,1,0:T(8,128)(2,1)}, u32[]{:S(2)}) copy-start(bf16[1,1,128,2048]{3,2,1,0:T(8,128)(2,1)} %param.8) | copy-start | bytes 1572868
  84.4 13.4 %copy-start.6 = (bf16[1,1,128,2048]{3,2,1,0:T(8,128)(2,1)S(1)}, bf16[1,1,128,2048]{3,2,1,0:T(8,128)(2,1)}, u32[]{:S(2)}) copy-start(bf16[1,1,128,2048]{3,2,1,0:T(8,128)(2,1)} %param.7) | copy-start | bytes 1572868
  84.4 108.6 %all-to-all-start = ((bf16[64,16,2048]{2,1,0:T(8,128)(2,1)}), bf16[64,16,2048]{2,1,0:T(8,128)(2,1)}, u32[]{:S(2)}, u32[]{:S(2)}) async-start(bf16[64,16,2048]{2,1,0:T(8,128)(2,1)} %bitcast.129), calls=%async_computation | async-start | bytes 8388608 | tf_op jit(solution)/shard_map/all_to_all | solution.py:67
  195.5 100.7 %all-to-all-start.1 = ((bf16[64,16,2048]{2,1,0:T(8,128)(2,1)}), bf16[64,16,2048]{2,1,0:T(8,128)(2,1)}, u32[]{:S(2)}, u32[]{:S(2)}) async-start(bf16[64,16,2048]{2,1,0:T(8,128)(2,1)} %bitcast.128), calls=%async_computation.1 | async-start | bytes 8388608 | tf_op jit(solution)/shard_map/all_to_all | solution.py:66
  202.5 100.8 %all-gather.8.cloned.1.call-start = ((), (), s32[]{:S(2)}) async-start(), calls=%async_computation.6 | async-start | bytes 1572864 | tf_op jit(solution)/shard_map/all_gather | solution.py:74
  203.3 102.9 %all-gather.6.cloned.1.call-start = ((), (), s32[]{:S(2)}) async-start(), calls=%async_computation.5 | async-start | bytes 1572864 | tf_op jit(solution)/shard_map/all_gather | solution.py:75
  204.0 104.9 %all-gather.4.cloned.1.call-start = ((), (), s32[]{:S(2)}) async-start(), calls=%async_computation.4 | async-start | bytes 1572864 | tf_op jit(solution)/shard_map/all_gather | solution.py:76
  308.9 3.2 copy-start.3
  312.1 1.2 copy-start.4
  322.9 100.7 %all-to-all-start.2 = ((bf16[64,16,2048]{2,1,0:T(8,128)(2,1)}), bf16[64,16,2048]{2,1,0:T(8,128)(2,1)}, u32[]{:S(2)}, u32[]{:S(2)}) async-start(bf16[64,16,2048]{2,1,0:T(8,128)(2,1)} %bitcast.130), calls=%async_computation.2 | async-start | bytes 8388608 | tf_op jit(solution)/shard_map/all_to_all | solution.py:100
  329.9 410.5 %reduce-scatter.2.cloned.1.call-start = ((), (), s32[]{:S(2)}) async-start(), calls=%async_computation.7 | async-start | bytes 4718592 | tf_op jit(solution)/shard_map/reduce_scatter | solution.py:119
  330.7 1.6 copy-start.2
  438.6 307.5 %collective-permute-start = (bf16[1,1,128,2048]{3,2,1,0:T(8,128)(2,1)S(1)}, bf16[1,1,128,2048]{3,2,1,0:T(8,128)(2,1)S(1)}, u32[]{:S(2)}, u32[]{:S(2)}) collective-permute-start(bf16[1,1,128,2048]{3,2,1,0:T(8,128)(2,1)S(1)} %fusion.22), channel_id=1, source_target_pairs={{128,0},{129,1},{130,2},{131,3},{132,4},{133,5},{134,6},{135,7},{1... | collective-permute-start | bytes 1572872 | tf_op jit(solution)/shard_map/ppermute | solution.py:12
  743.5 3.4 copy-start.1
Sparse Core Ops, SparseCore 0:
  205.2 15.1 all-gather.7
  222.2 15.6 all-gather.5
  239.7 15.6 all-gather.3
  335.2 16.9 reduce-scatter.1
where the time goes:
time: 763 us; the launch traced here: 753 us
  blocking collectives  300 us (39%)
  waiting for transfers between devices  268 us (35%)
  local copies, waits for them, and re-layouts  71.1 us (9%)
  other arithmetic  57.5 us (8%)
  starting transfers between devices  28.8 us (4%)
  between operations  14.2 us (2%)
  matrix products  13.9 us (2%)
    psum x1, blocking collectives, on_device(): gate_grad = lax.psum(partial_gates, 'expert')[None, None]  300 us
    all_to_all x1, waiting for transfers between devices, on_device(): lax.all_to_all(sent_grads, 'expert', split_axis=0, concat_axis=0, tiled=T...  93.8 us
    all_to_all x1, waiting for transfers between devices, on_device(): lax.all_to_all(returning.reshape(expert_devices, slot_count, model_width)...  88.4 us
    all_to_all x1, waiting for transfers between devices, on_device(): lax.all_to_all(sent_rows, 'expert', split_axis=0, concat_axis=0, tiled=True)  83.2 us
    unnamed x26, local copies, waits for them, and re-layouts  35.2 us
    another operation x2, other arithmetic  34.1 us
  transfers between devices with their start and end apart: 8, of which 3 were waited for; matrix products, arithmetic and copies ran while one was open for 6% of the time, Pallas kernels for 0%

commit v1 on v0

v1 whole, which is shorter than its diff:
```python
import jax
import jax.numpy as jnp
from jax import lax
from jax.experimental import pallas as pl
from jax.experimental.pallas import tpu as pltpu
from jax.sharding import PartitionSpec as P

MESH = pl.DeviceIdType.MESH
BF16 = jnp.bfloat16
F32 = jnp.float32

TOK = 128
WIDTH = 2048
QUARTER = 512
HIDDEN = 256
RANKS = 64
MSG = 16
CAP = 512
HALF = 1024


def dot(left, right):
    return lax.dot_general(left, right, (((1,), (0,)), ((), ())), preferred_element_type=F32)


def dot_last(left, right):
    return lax.dot_general(left, right, (((1,), (1,)), ((), ())), preferred_element_type=F32)


def dot_first(left, right):
    return lax.dot_general(left, right, (((0,), (0,)), ((), ())), preferred_element_type=F32)


def iota(shape, dim):
    return lax.broadcasted_iota(jnp.int32, shape, dim)


def ones_if(condition):
    return jnp.where(condition, 1.0, 0.0).astype(BF16)


def rows_at(index, size):
    return pl.ds(pl.multiple_of(index * size, size), size)


def flip(rank):
    return rank + 1 - 2 * (rank % 2)


def token_selector(sel, block, pair):
    bound = block * TOK + iota((TOK, CAP), 0)
    first = sel[pl.ds(2 * pair, 1), :]
    second = sel[pl.ds(2 * pair + 1, 1), :]
    below = jnp.concatenate([ones_if(first < bound), ones_if(second < bound)], axis=1)
    same = jnp.concatenate([ones_if(first == bound), ones_if(second == bound)], axis=1)
    halves = ones_if((iota((2 * CAP, TOK), 0) < CAP) == (iota((2 * CAP, TOK), 1) < 64))
    rank = dot(below, halves).astype(jnp.int32)
    taken = dot(same, halves)
    start = rank[0:1, :]
    lane = iota((TOK, TOK), 1) & 63
    hit = (taken > 0.5) & ((rank & 3) == (lane >> 4)) & (((rank - start) >> 2) == (lane & 3))
    return jnp.where(hit, 1.0, 0.0)


def slot_selector(mine, member, part):
    row = part * TOK + iota((TOK, CAP), 0)
    bound = (row >> 4) * TOK
    ones = jnp.ones((CAP, TOK), F32).astype(BF16)
    before = dot(ones_if(mine < bound), ones).astype(jnp.int32)
    after = dot(ones_if(mine < bound + TOK), ones).astype(jnp.int32)
    slot = iota((TOK, TOK), 0) & 3
    index = 4 * slot + ((member + 1024 - before) & 3)
    hit = (index < after - before) & (((before + index) >> 2) == iota((TOK, TOK), 1))
    return jnp.where(hit, 1.0, 0.0)


def quarter_of_row(quarter, rows, lanes):
    return ones_if(((iota((rows, lanes), 0) >> 2) & 3) == quarter)


def quarter_of_lane(quarter, rows, lanes):
    return ones_if(((iota((rows, lanes), 1) >> 2) & 3) == quarter)


def spread_rows(selector, source, target):
    def step(i, carry):
        chosen = selector[rows_at(i, 256), :]
        total = None
        for quarter in range(4):
            term = dot(
                chosen * quarter_of_row(quarter, 256, TOK),
                source[:, quarter * QUARTER : (quarter + 1) * QUARTER],
            )
            total = term if total is None else total + term
        target[rows_at(i, 256), :] = total.astype(BF16)
        return carry

    lax.fori_loop(0, 4, step, 0)


def kernel(
    rows,
    grads,
    sel,
    gates,
    gate_w,
    up_w,
    down_w,
    incoming,
    gate_grad,
    gate_wg,
    up_wg,
    down_wg,
    send_rows,
    send_grads,
    recv_rows,
    recv_grads,
    send_back,
    recv_back,
    rows_all,
    grads_all,
    gated_all,
    gate_full,
    up_full,
    down_full,
    gate_pre,
    up_pre,
    act_all,
    ggp_all,
    gup_all,
    to_slot,
    from_token,
    place_of,
    place_from,
    gate_col,
    part_col,
    place_mat,
    part_own,
    part_send,
    part_recv,
    summed,
    term_gate,
    term_up,
    term_down,
    send_tgate,
    send_tup,
    send_tdown,
    recv_tgate,
    recv_tup,
    recv_tdown,
    gsend,
    grecv,
    gsum,
    gall,
    combined,
    arrived,
    s_a2a,
    r_a2a,
    s_w,
    r_w,
    s_rows,
    r_rows,
    s_grads,
    r_grads,
    s_part,
    r_part,
    s_term,
    r_term,
    s_gate,
    r_gate,
    s_spread,
    r_spread,
    s_fin,
    r_fin,
):
    section = lax.axis_index("section")
    me = lax.axis_index("expert")
    dp = lax.axis_index("dp")
    plane = me // 8
    spot = me % 8
    owner = me // 4
    member = me % 4
    mx = flip(member)
    my = (member + 2) % 4
    md = flip(my)
    base = owner * 4
    near_x = base + mx
    near_y = base + my
    far = base + md
    mirror = flip(me)

    barrier = pltpu.get_barrier_semaphore()

    def greet(i, carry):
        pl.semaphore_signal(
            barrier, inc=1, device_id={"expert": (me + i) % RANKS}, device_id_type=MESH
        )
        return carry

    lax.fori_loop(1, RANKS, greet, 0)
    pl.semaphore_signal(barrier, inc=1, device_id={"dp": 1 - dp}, device_id_type=MESH)
    pl.semaphore_signal(
        barrier, inc=1, device_id={"section": 1 - section, "expert": mirror}, device_id_type=MESH
    )

    def make_to_slot(pair, carry):
        tile = token_selector(sel, me, pair)
        to_slot[rows_at(pair, TOK), :] = jnp.transpose(tile).astype(BF16)
        return carry

    lax.fori_loop(0, 8, make_to_slot, 0)
    spread_rows(to_slot, rows, send_rows)

    pl.semaphore_wait(barrier, RANKS + 1)

    def remote(source, target, s_sem, r_sem, where):
        return pltpu.make_async_remote_copy(
            src_ref=source,
            dst_ref=target,
            send_sem=s_sem,
            recv_sem=r_sem,
            device_id=where,
            device_id_type=MESH,
        )

    def exchange(source, target, index, mirrored):
        def step(i, carry):
            turn = i % 8
            dz = (turn % 2) * ((turn + 1) // 2) + (1 - turn % 2) * ((8 - turn // 2) % 8)
            to = ((plane + dz) % 8) * 8 + (spot + i // 8) % 8
            block = flip(to) if mirrored else to
            remote(
                source.at[rows_at(block, MSG)],
                target.at[rows_at(me, MSG)],
                s_a2a.at[index],
                r_a2a.at[index],
                {"expert": to},
            ).start()
            return carry

        lax.fori_loop(1, RANKS, step, 0)
        block = flip(me) if mirrored else me
        target[rows_at(me, MSG), :] = source[rows_at(block, MSG), :]

    def drain(ref, sem):
        view = ref.at[pl.ds(0, (RANKS - 1) * MSG)]
        pltpu.make_async_copy(view, view, sem).wait()

    def await_copy(view, sem):
        pltpu.make_async_copy(view, view, sem).wait()

    exchange(send_rows, recv_rows, 0, False)

    partner = {"dp": 1 - dp}
    weight_copies = [
        remote(gate_w, gate_full.at[rows_at(dp, HALF)], s_w.at[0], r_w.at[0], partner),
        remote(up_w, up_full.at[rows_at(dp, HALF)], s_w.at[1], r_w.at[1], partner),
        remote(down_w, down_full.at[dp], s_w.at[2], r_w.at[2], partner),
    ]
    for copy in weight_copies:
        copy.start()

    spread_rows(to_slot, grads, send_grads)
    exchange(send_grads, recv_grads, 1, False)

    gate_full[rows_at(dp, HALF), :] = gate_w[...]
    up_full[rows_at(dp, HALF), :] = up_w[...]
    down_full[dp] = down_w[...]

    mine = sel[pl.ds(owner, 1), :]

    def make_place(part, carry):
        tile = slot_selector(mine, member, part)
        place_of[rows_at(part, TOK), :] = tile.astype(BF16)
        place_from[:, rows_at(part, TOK)] = jnp.transpose(tile).astype(BF16)
        return carry

    lax.fori_loop(0, 8, make_place, 0)

    def make_from_token(pair, carry):
        from_token[:, rows_at(pair, TOK)] = token_selector(sel, mirror, pair).astype(BF16)
        return carry

    lax.fori_loop(0, 8, make_from_token, 0)

    across = iota((CAP, CAP), 1)
    down = iota((CAP, CAP), 0)
    mine_f = mine.astype(F32)
    mine_col = jnp.sum(jnp.where(across == down, mine_f, 0.0), axis=1, keepdims=True)
    rank = jnp.sum(jnp.where(mine_col < mine_f, 1.0, 0.0), axis=0, keepdims=True).astype(jnp.int32)
    place = (rank & 3) * TOK + (rank >> 2)
    place_mat[...] = jnp.where(place == down, 1.0, 0.0)
    gate_col[...] = jnp.sum(
        jnp.where(place_mat[...] > 0.5, gates[pl.ds(owner, 1), :], 0.0), axis=1, keepdims=True
    )

    def compact(source, target):
        view = target.at[rows_at(member, TOK)]
        for quarter in range(4):
            chosen = place_from[...] * quarter_of_lane(quarter, TOK, RANKS * MSG)
            view[:, quarter * QUARTER : (quarter + 1) * QUARTER] = dot(chosen, source[...]).astype(
                BF16
            )

    low, high = pl.ds(0, HALF), pl.ds(HALF, HALF)

    def gather_own(ref, s, r):
        own = ref.at[rows_at(member, TOK)]
        remote(own, own, s.at[0], r.at[0], {"expert": near_x}).start()
        remote(own, own, s.at[1], r.at[1], {"expert": near_y}).start()

    def gather_forward(ref, s, r):
        from_x = ref.at[rows_at(mx, TOK)]
        await_copy(from_x, r.at[0])
        view = ref.at[rows_at(mx, TOK), low]
        remote(view, view, s.at[2], r.at[2], {"expert": near_y}).start()
        from_y = ref.at[rows_at(my, TOK)]
        await_copy(from_y, r.at[1])
        view = ref.at[rows_at(my, TOK), high]
        remote(view, view, s.at[3], r.at[3], {"expert": near_x}).start()

    def gather_far(ref, r):
        await_copy(ref.at[rows_at(md, TOK), low], r.at[2])
        await_copy(ref.at[rows_at(md, TOK), high], r.at[3])

    def gather_sent(ref, s):
        await_copy(ref.at[rows_at(member, TOK)], s.at[0])
        await_copy(ref.at[rows_at(member, TOK)], s.at[1])
        await_copy(ref.at[rows_at(mx, TOK), low], s.at[2])
        await_copy(ref.at[rows_at(my, TOK), high], s.at[3])

    def forward(block):
        at = rows_at(block, TOK)
        gate_pre[at, :] = dot(rows_all[at, :], gate_full[...])
        up_pre[at, :] = dot(rows_all[at, :], up_full[...])

    def backward(block):
        at = rows_at(block, TOK)
        grad = grads_all[at, :]
        upstream = dot_last(grad[:, :HALF], down_full[0]) + dot_last(grad[:, HALF:], down_full[1])
        pre, up = gate_pre[at, :], up_pre[at, :]
        sigmoid = jax.nn.sigmoid(pre)
        swish = pre * sigmoid
        activation = (swish * up).astype(BF16)
        gate = gate_col[at, :]
        part_col[at, :] = jnp.sum(activation.astype(F32) * upstream, axis=1, keepdims=True)
        scaled = gate * upstream
        ggp = (scaled * up * sigmoid * (1.0 + pre * (1.0 - sigmoid))).astype(BF16)
        gup = (scaled * swish).astype(BF16)
        act_all[at, :] = activation
        ggp_all[at, :] = ggp
        gup_all[at, :] = gup
        gated_all[at, :] = (gate * grad.astype(F32)).astype(BF16)
        return dot_last(ggp, gate_full[...]) + dot_last(gup, up_full[...])

    drain(recv_rows, r_a2a.at[0])
    compact(recv_rows, rows_all)
    gather_own(rows_all, s_rows, r_rows)
    for i, view in enumerate(
        (gate_full.at[rows_at(1 - dp, HALF)], up_full.at[rows_at(1 - dp, HALF)], down_full.at[1 - dp])
    ):
        await_copy(view, r_w.at[i])
    forward(member)
    gather_forward(rows_all, s_rows, r_rows)
    forward(mx)
    forward(my)
    gather_far(rows_all, r_rows)
    forward(md)

    drain(recv_grads, r_a2a.at[1])
    compact(recv_grads, grads_all)
    gather_own(grads_all, s_grads, r_grads)
    part_own[...] = backward(member)
    gather_forward(grads_all, s_grads, r_grads)
    part_copies = [
        remote(part_send.at[i], part_recv.at[i], s_part.at[i], r_part.at[i], {"expert": to})
        for i, to in enumerate((near_x, near_y, far))
    ]
    part_send[0] = backward(mx).astype(BF16)
    part_copies[0].start()
    part_send[1] = backward(my).astype(BF16)
    part_copies[1].start()
    gather_far(grads_all, r_grads)
    part_send[2] = backward(md).astype(BF16)
    part_copies[2].start()

    part_row = jnp.sum(place_mat[...] * part_col[...], axis=0, keepdims=True)
    gsend[...] = jnp.zeros((8, TOK), F32)
    for i in range(4):
        gsend[i : i + 1, :] = part_row[:, i * TOK : (i + 1) * TOK]
    gate_copies = [
        remote(gsend, grecv.at[i], s_gate.at[i], r_gate.at[i], {"expert": to})
        for i, to in enumerate((near_x, near_y, far))
    ]
    for copy in gate_copies:
        copy.start()

    def weight_terms(half, gate_to, up_to, down_to):
        def step(i, carry):
            columns = pl.ds(pl.multiple_of(half * HALF + i * 256, 256), 256)
            left = rows_all[:, columns]
            gate_to[rows_at(i, 256), :] = dot_first(left, ggp_all[...]).astype(BF16)
            up_to[rows_at(i, 256), :] = dot_first(left, gup_all[...]).astype(BF16)
            down_to[:, rows_at(i, 256)] = dot_first(act_all[...], gated_all[:, columns]).astype(BF16)
            return carry

        lax.fori_loop(0, 4, step, 0)

    weight_terms(1 - dp, send_tgate, send_tup, send_tdown)
    term_copies = [
        remote(send_tgate, recv_tgate, s_term.at[0], r_term.at[0], partner),
        remote(send_tup, recv_tup, s_term.at[1], r_term.at[1], partner),
        remote(send_tdown, recv_tdown, s_term.at[2], r_term.at[2], partner),
    ]
    for copy in term_copies:
        copy.start()

    for copy in gate_copies:
        copy.wait_recv()
    gsum[...] = (gsend[...] + grecv[0]) + (grecv[1] + grecv[2])

    def spread_gate(i, carry):
        to = ((owner + i) % 16) * 4 + member
        remote(gsum, gall.at[rows_at(owner, 8)], s_spread, r_spread, {"expert": to}).start()
        return carry

    lax.fori_loop(1, 16, spread_gate, 0)
    gall[rows_at(owner, 8), :] = gsum[...]

    weight_terms(dp, term_gate, term_up, term_down)

    for copy in part_copies:
        copy.wait_recv()
    summed[...] = (
        (part_own[...] + part_recv[0].astype(F32))
        + (part_recv[1].astype(F32) + part_recv[2].astype(F32))
    ).astype(BF16)
    spread_rows(place_of, summed, send_back)
    exchange(send_back, recv_back, 2, True)

    for copy in term_copies:
        copy.wait_recv()
    gate_wg[...] = (term_gate[...].astype(F32) + recv_tgate[...].astype(F32)) * 0.5
    up_wg[...] = (term_up[...].astype(F32) + recv_tup[...].astype(F32)) * 0.5
    down_wg[...] = (term_down[...].astype(F32) + recv_tdown[...].astype(F32)) * 0.5

    others = gall.at[pl.ds(0, 15 * 8)]
    await_copy(others, r_spread)
    for e in range(16):
        for i in range(4):
            gate_grad[e : e + 1, i * TOK : (i + 1) * TOK] = gall[e * 8 + i : e * 8 + i + 1, :]

    drain(recv_back, r_a2a.at[2])
    for quarter in range(4):
        chosen = from_token[...] * quarter_of_lane(quarter, TOK, RANKS * MSG)
        combined[:, quarter * QUARTER : (quarter + 1) * QUARTER] = dot(
            chosen, recv_back[...]
        ).astype(BF16)
    last = remote(combined, arrived, s_fin, r_fin, {"section": 0, "expert": mirror})

    @pl.when(section == 1)
    def _():
        last.start()
        incoming[...] = jnp.zeros((TOK, WIDTH), BF16)
        last.wait_send()

    @pl.when(section == 0)
    def _():
        last.wait_recv()
        incoming[...] = arrived[...]

    drain(send_rows, s_a2a.at[0])
    drain(send_grads, s_a2a.at[1])
    drain(send_back, s_a2a.at[2])
    for copy in (*weight_copies, *part_copies, *gate_copies, *term_copies):
        copy.wait_send()
    gather_sent(rows_all, s_rows)
    gather_sent(grads_all, s_grads)
    await_copy(others, s_spread)


def on_device(
    layer_input, grad_output, selections, gate_values, gate_weight, up_weight, down_weight
):
    vmem = pl.BlockSpec(memory_space=pltpu.VMEM)
    shape = jax.ShapeDtypeStruct
    dma = pltpu.SemaphoreType.DMA
    message = pltpu.VMEM((RANKS * MSG, QUARTER), BF16)
    wide = pltpu.VMEM((CAP, WIDTH), BF16)
    pre = pltpu.VMEM((CAP, HIDDEN), F32)
    post = pltpu.VMEM((CAP, HIDDEN), BF16)
    tall = pltpu.VMEM((RANKS * MSG, TOK), BF16)
    flat = pltpu.VMEM((TOK, RANKS * MSG), BF16)
    tile = pltpu.VMEM((HALF, HIDDEN), BF16)
    tile_t = pltpu.VMEM((HIDDEN, HALF), BF16)
    outs = pl.pallas_call(
        kernel,
        out_shape=(
            shape((TOK, WIDTH), BF16),
            shape((16, CAP), F32),
            shape((HALF, HIDDEN), F32),
            shape((HALF, HIDDEN), F32),
            shape((HIDDEN, HALF), F32),
        ),
        in_specs=[vmem] * 7,
        out_specs=(vmem,) * 5,
        scratch_shapes=[
            message,
            message,
            message,
            message,
            message,
            message,
            wide,
            wide,
            wide,
            pltpu.VMEM((WIDTH, HIDDEN), BF16),
            pltpu.VMEM((WIDTH, HIDDEN), BF16),
            pltpu.VMEM((2, HIDDEN, HALF), BF16),
            pre,
            pre,
            post,
            post,
            post,
            tall,
            flat,
            tall,
            flat,
            pltpu.VMEM((CAP, 1), F32),
            pltpu.VMEM((CAP, 1), F32),
            pltpu.VMEM((CAP, CAP), F32),
            pltpu.VMEM((TOK, WIDTH), F32),
            pltpu.VMEM((3, TOK, WIDTH), BF16),
            pltpu.VMEM((3, TOK, WIDTH), BF16),
            pltpu.VMEM((TOK, WIDTH), BF16),
            tile,
            tile,
            tile_t,
            tile,
            tile,
            tile_t,
            tile,
            tile,
            tile_t,
            pltpu.VMEM((8, TOK), F32),
            pltpu.VMEM((3, 8, TOK), F32),
            pltpu.VMEM((8, TOK), F32),
            pltpu.VMEM((16 * 8, TOK), F32),
            pltpu.VMEM((TOK, WIDTH), BF16),
            pltpu.VMEM((TOK, WIDTH), BF16),
            dma((3,)),
            dma((3,)),
            dma((3,)),
            dma((3,)),
            dma((4,)),
            dma((4,)),
            dma((4,)),
            dma((4,)),
            dma((3,)),
            dma((3,)),
            dma((3,)),
            dma((3,)),
            dma((3,)),
            dma((3,)),
            dma,
            dma,
            dma,
            dma,
        ],
        compiler_params=pltpu.CompilerParams(
            collective_id=0, has_side_effects=True, vmem_limit_bytes=56 * 2**20
        ),
        cost_estimate=pl.CostEstimate(
            flops=8_000_000_000, bytes_accessed=8_000_000, transcendentals=131072
        ),
    )(
        layer_input[0, 0],
        grad_output[0, 0],
        selections[0, 0],
        gate_values[0, 0],
        gate_weight[0, 0],
        up_weight[0, 0],
        down_weight[0, 0],
    )
    return tuple(out[None, None] for out in outs)


def solution(mesh):
    return jax.shard_map(
        on_device,
        mesh=mesh,
        in_specs=(
            P("section", "dp", "expert", None),
            P("section", "dp", "expert", None),
            P("section", "dp", None, None),
            P("section", "dp", None, None),
            P("section", "expert", "dp", None),
            P("section", "expert", "dp", None),
            P("section", "expert", None, "dp"),
        ),
        out_specs=(
            P("section", "dp", "expert", None),
            P("section", "dp", None, None),
            P("section", "expert", "dp", None),
            P("section", "expert", "dp", None),
            P("section", "expert", None, "dp"),
        ),
        check_vma=False,
    )
```

time: 763 us -> 159 us (0.21); the launches traced: 753 us -> 159 us
  blocking collectives: 300 us -> 0 us
  waiting for transfers between devices: 268 us -> 0 us
  Pallas kernels: 0 us -> 150 us
  local copies, waits for them, and re-layouts: 71.1 us -> 7.52 us
  other arithmetic: 57.5 us -> 0 us
  starting transfers between devices: 28.8 us -> 0 us
  matrix products: 13.9 us -> 0 us
  between operations: 14.2 us -> 0.65 us
    psum x1 -> x0, blocking collectives: 300 us -> none  [on_device(): gate_grad = lax.psum(partial_gates, 'expert')[None, None]]
    all_to_all x3 -> x0, waiting for transfers between devices: 265 us -> none  [the longest x1 93.8 us: on_device(): lax.all_to_all(sent_grads, 'expert', split_axis=0, concat_axis=0, tiled=T...]
    pallas_call x0 -> x1, Pallas kernels: none -> 150 us  [on_device(): pl.pallas_call(kernel, out_shape=(shape((TOK, WIDTH), BF16), shape((16, C...]
    another operation x2 -> x0, other arithmetic: 34.1 us -> none
    unnamed x26 -> x11, local copies, waits for them, and re-layouts: 35.2 us -> 7.52 us
    all_to_all x3 -> x0, starting transfers between devices: 27.4 us -> none  [the longest x1 13.3 us: on_device(): lax.all_to_all(sent_grads, 'expert', split_axis=0, concat_axis=0, tiled=T...]
    gather x4 -> x0, local copies, waits for them, and re-layouts: 18 us -> none  [the longest x1 8.14 us: on_device(): rows_grad = got_grads[flat_slot]]
    scatter-add x1 -> x0, other arithmetic: 14.9 us -> none  [on_device(): summed = jnp.zeros((token_count + 1, model_width), jnp.float32).at[send_t...]
  transfers between devices with their start and end apart: 8 -> 0, of which waited for: 3 -> 0; matrix products, arithmetic and copies ran while one was open for 6% -> 0% of each run, Pallas kernels for 0% -> 0%
where the time goes in v1:
time: 159 us
  Pallas kernels  150 us (94%)
  local copies, waits for them, and re-layouts  7.52 us (5%)
    pallas_call x1, Pallas kernels, on_device(): pl.pallas_call(kernel, out_shape=(shape((TOK, WIDTH), BF16), shape((16, C...  150 us
    unnamed x11, local copies, waits for them, and re-layouts  7.52 us

profile of v1, /device:TPU:8, one launch (start us, length us, event | category | flops | bytes accessed | tf_op | source)
XLA Modules:
  0.0 158.7 jit_solution(402114182357765752)
XLA Ops:
  0.6 150.5 %shard_map.110 = (bf16[128,2048]{1,0:T(8,128)(2,1)}, f32[16,512]{1,0:T(8,128)}, f32[1024,256]{1,0:T(8,128)}, f32[1024,256]{1,0:T(8,128)}, f32[256,1024]{1,0:T(8,128)}) custom-call(bf16[128,2048]{1,0:T(8,128)(2,1)} %bitcast.17, bf16[128,2048]{1,0:T(8,128)(2,1)} %bitcast.18, s32[16,512]{1,0:T(8,128)} %bitcast.22, f32[16,512]{1,0:T(8,128)} %bitcast.23, ...), custom_call_target="tpu_custom_call" | custom-call | flops 8000000000 | bytes 8000000 | tf_op jit(solution)/shard_map/pallas_call | solution.py:496
  151.1 0.0 copy-start.2
  151.1 2.0 %copy.17 = bf16[1,1,128,2048]{3,2,1,0:T(8,128)(2,1)} copy(bf16[1,1,128,2048]{3,2,1,0:T(8,128)(2,1)} %bitcast.15) | data formatting | bytes 1048576
  153.1 1.4 copy.18
  154.5 0.0 copy-done.2
  154.5 0.0 copy-start.1
  154.5 1.0 copy.19
  155.5 0.6 copy-done.1
  156.1 0.0 copy-start
  156.1 1.0 copy.20
  157.1 0.6 copy-done
  157.7 1.0 copy.21
Async XLA Ops:
  151.1 3.4 %copy-start.2 = (f32[1024,256]{1,0:T(8,128)S(1)}, f32[1024,256]{1,0:T(8,128)}, u32[]{:S(2)}) copy-start(f32[1024,256]{1,0:T(8,128)} %get-tuple-element.12) | copy-start | bytes 3145732
  154.5 1.6 %copy-start.1 = (f32[1024,256]{1,0:T(8,128)S(1)}, f32[1024,256]{1,0:T(8,128)}, u32[]{:S(2)}) copy-start(f32[1024,256]{1,0:T(8,128)} %get-tuple-element.13) | copy-start | bytes 3145732
  156.1 1.6 %copy-start = (f32[256,1024]{1,0:T(8,128)S(1)}, f32[256,1024]{1,0:T(8,128)}, u32[]{:S(2)}) copy-start(f32[256,1024]{1,0:T(8,128)} %get-tuple-element.14) | copy-start | bytes 3145732

commit v2 on v1

v2 whole, which is shorter than its diff:
```python
import jax
import jax.numpy as jnp
from jax import lax
from jax.experimental import pallas as pl
from jax.experimental.pallas import tpu as pltpu
from jax.sharding import PartitionSpec as P

MESH = pl.DeviceIdType.MESH
BF16 = jnp.bfloat16
F32 = jnp.float32

TOK = 128
WIDTH = 2048
HIDDEN = 256
RANKS = 64
MSG = 16
ALL = RANKS * MSG
CAP = 512
HALF = 1024
PIECES = 4
PIECE = WIDTH // PIECES


def dot(left, right):
    return lax.dot_general(left, right, (((1,), (0,)), ((), ())), preferred_element_type=F32)


def dot_last(left, right):
    return lax.dot_general(left, right, (((1,), (1,)), ((), ())), preferred_element_type=F32)


def dot_first(left, right):
    return lax.dot_general(left, right, (((0,), (0,)), ((), ())), preferred_element_type=F32)


def iota(shape, dim):
    return lax.broadcasted_iota(jnp.int32, shape, dim)


def one_if(condition):
    return jnp.where(condition, 1.0, 0.0)


def ones_if(condition):
    return one_if(condition).astype(BF16)


def rows_at(index, size):
    return pl.ds(pl.multiple_of(index * size, size), size)


def flip(rank):
    return rank + 1 - 2 * (rank % 2)


def slot_codes(sel, columns, block):
    tokens = (block * TOK + iota((CAP, TOK), 1)).astype(F32)
    taken = jnp.concatenate(
        [
            jnp.sum(one_if(columns[:, e : e + 1] == tokens), axis=0, keepdims=True)
            for e in range(16)
        ],
        axis=0,
    )
    upper = ones_if(iota((TOK, TOK), 0) < iota((TOK, TOK), 1))
    index = dot(taken.astype(BF16), upper).astype(jnp.int32)
    start = jnp.sum(one_if(sel < block * TOK), axis=1, keepdims=True).astype(jnp.int32)
    return jnp.where(taken > 0.5, ((start + index) & 3) * 16 + (index >> 2), -1)


def slot_selector(mine, member, part):
    row = part * TOK + iota((TOK, CAP), 0)
    bound = (row >> 4) * TOK
    ones = jnp.ones((CAP, TOK), F32).astype(BF16)
    before = dot(ones_if(mine < bound), ones).astype(jnp.int32)
    after = dot(ones_if(mine < bound + TOK), ones).astype(jnp.int32)
    slot = iota((TOK, TOK), 0) & 3
    index = 4 * slot + ((member + 1024 - before) & 3)
    hit = (index < after - before) & (((before + index) >> 2) == iota((TOK, TOK), 1))
    return one_if(hit)


def quarter(shape, dim, which):
    return ((iota(shape, dim) >> 2) & 3) == which


def spread_rows(selector, source, start, width, target):
    part = width // 4

    def step(i, carry):
        stacked = jnp.concatenate(
            [source[:, start + s * part : start + (s + 1) * part] for s in range(4)], axis=0
        )
        target[rows_at(i, 256), :] = dot(selector[rows_at(i, 256), :], stacked).astype(BF16)
        return carry

    lax.fori_loop(0, 4, step, 0)


def kernel(
    rows,
    grads,
    sel,
    gates,
    gate_w,
    up_w,
    down_w,
    incoming,
    gate_grad,
    gu_own,
    gu_other,
    down_own,
    down_other,
    send_fwd,
    recv_fwd,
    send_back,
    recv_back,
    rows_all,
    grads_all,
    gated_all,
    gu_full,
    down_full,
    pre_all,
    ups_all,
    act_all,
    act_t,
    gg_all,
    codes,
    to_slot,
    from_token,
    place_of,
    place_from,
    gate_col,
    part_col,
    place_mat,
    part_own,
    part_send,
    part_recv,
    summed,
    gu_send,
    gu_keep,
    down_send,
    down_keep,
    gsend,
    grecv,
    gsum,
    gall,
    combined,
    arrived,
    s_fwd,
    r_fwd,
    s_back,
    r_back,
    s_w,
    r_w,
    s_own,
    s_gather,
    r_gather,
    s_part,
    r_part,
    s_term,
    r_term,
    s_out,
    s_gate,
    r_gate,
    s_spread,
    r_spread,
    s_fin,
    r_fin,
):
    section = lax.axis_index("section")
    me = lax.axis_index("expert")
    dp = lax.axis_index("dp")
    plane = me // 8
    spot = me % 8
    owner = me // 4
    member = me % 4
    mx = flip(member)
    my = (member + 2) % 4
    md = flip(my)
    near_x = owner * 4 + mx
    near_y = owner * 4 + my
    far = owner * 4 + md
    mirror = flip(me)

    def remote(source, target, s_sem, r_sem, where):
        return pltpu.make_async_remote_copy(
            src_ref=source,
            dst_ref=target,
            send_sem=s_sem,
            recv_sem=r_sem,
            device_id=where,
            device_id_type=MESH,
        )

    def await_copy(view, sem):
        pltpu.make_async_copy(view, view, sem).wait()

    barrier = pltpu.get_barrier_semaphore()

    def greet(i, carry):
        pl.semaphore_signal(
            barrier, inc=1, device_id={"expert": (me + i) % RANKS}, device_id_type=MESH
        )
        return carry

    lax.fori_loop(1, RANKS, greet, 0)
    pl.semaphore_signal(barrier, inc=1, device_id={"dp": 1 - dp}, device_id_type=MESH)
    pl.semaphore_signal(
        barrier, inc=1, device_id={"section": 1 - section, "expert": mirror}, device_id_type=MESH
    )

    gate_cols, up_cols = pl.ds(0, HIDDEN), pl.ds(HIDDEN, HIDDEN)
    weight_views = [
        (gate_w, gu_full.at[rows_at(dp, HALF), gate_cols]),
        (up_w, gu_full.at[rows_at(dp, HALF), up_cols]),
        (down_w, down_full.at[dp]),
    ]
    own_copies = [
        pltpu.make_async_copy(source, target, s_own.at[i])
        for i, (source, target) in enumerate(weight_views)
    ]
    for copy in own_copies:
        copy.start()

    columns = jnp.transpose(sel[...].astype(F32))
    codes[...] = slot_codes(sel[...], columns, me)

    def make_to_slot(e, carry):
        line = iota((64, TOK), 0)
        hit = codes[pl.ds(e, 1), :] == line - (line & 12)
        for s in range(4):
            to_slot[rows_at(e, 64), s * TOK : (s + 1) * TOK] = ones_if(
                hit & quarter((64, TOK), 0, s)
            )
        return carry

    lax.fori_loop(0, 16, make_to_slot, 0)
    spread_rows(to_slot, rows, 0, HALF, send_fwd.at[0])

    pl.semaphore_wait(barrier, RANKS + 1)

    planes = [((plane + dz) % 8) * 8 for dz in (4, 1, 7, 2, 6, 3, 5, 0)]

    def exchange(source, target, s_sem, r_sem, mirrored):
        def send(to):
            block = flip(to) if mirrored else to
            remote(
                source.at[rows_at(block, MSG)],
                target.at[rows_at(me, MSG)],
                s_sem,
                r_sem,
                {"expert": to},
            ).start()

        def step(i, carry):
            place = (spot + i) % 8
            for start in planes:
                send(start + place)
            return carry

        for start in planes[:-1]:
            send(start + spot)
        lax.fori_loop(1, 8, step, 0)
        block = flip(me) if mirrored else me
        target[rows_at(me, MSG), :] = source[rows_at(block, MSG), :]

    def drain(ref, sem):
        await_copy(ref.at[pl.ds(0, (RANKS - 1) * MSG)], sem)

    def dispatch(i):
        exchange(send_fwd.at[i], recv_fwd.at[i], s_fwd.at[i], r_fwd.at[i], False)

    dispatch(0)
    partner = {"dp": 1 - dp}
    weight_copies = [
        remote(source, target, s_w.at[i], r_w.at[i], partner)
        for i, (source, target) in enumerate(weight_views)
    ]
    for copy in weight_copies:
        copy.start()
    spread_rows(to_slot, rows, HALF, HALF, send_fwd.at[1])
    dispatch(1)
    spread_rows(to_slot, grads, 0, HALF, send_fwd.at[2])
    dispatch(2)
    spread_rows(to_slot, grads, HALF, HALF, send_fwd.at[3])
    dispatch(3)

    mine = sel[pl.ds(owner, 1), :]

    def make_place(part, carry):
        tile = slot_selector(mine, member, part)
        turned = jnp.transpose(tile)
        for s in range(4):
            keep = slice(s * TOK, (s + 1) * TOK)
            place_of[rows_at(part, TOK), keep] = (
                tile * one_if(quarter((TOK, TOK), 0, s))
            ).astype(BF16)
            place_from[keep, rows_at(part, TOK)] = (
                turned * one_if(quarter((TOK, TOK), 1, s))
            ).astype(BF16)
        return carry

    lax.fori_loop(0, 8, make_place, 0)

    def make_tables():
        across = iota((CAP, CAP), 1)
        down = iota((CAP, CAP), 0)
        mine_f = mine.astype(F32)
        mine_col = jnp.sum(jnp.where(across == down, mine_f, 0.0), axis=1, keepdims=True)
        rank = jnp.sum(one_if(mine_col < mine_f), axis=0, keepdims=True).astype(jnp.int32)
        place = (rank & 3) * TOK + (rank >> 2)
        place_mat[...] = one_if(place == down)
        gate_col[...] = jnp.sum(
            jnp.where(place_mat[...] > 0.5, gates[pl.ds(owner, 1), :], 0.0), axis=1, keepdims=True
        )

    def make_from_token():
        codes[...] = slot_codes(sel[...], columns, mirror)

        def step(pair, carry):
            line = iota((TOK, TOK), 0)
            inner = line & 63
            wanted = jnp.where(
                line < 64, codes[pl.ds(2 * pair, 1), :], codes[pl.ds(2 * pair + 1, 1), :]
            )
            turned = jnp.transpose(one_if(wanted == inner - (inner & 12)))
            for s in range(4):
                from_token[s * TOK : (s + 1) * TOK, rows_at(pair, TOK)] = (
                    turned * one_if(quarter((TOK, TOK), 1, s))
                ).astype(BF16)
            return carry

        lax.fori_loop(0, 8, step, 0)

    def whole(i):
        return rows_all if i < 2 else grads_all

    def half_view(i, block, offset, width):
        return whole(i).at[rows_at(block, TOK), pl.ds((i % 2) * HALF + offset, width)]

    def gather_own(i):
        drain(recv_fwd.at[i], r_fwd.at[i])
        compacted = dot(place_from[...], recv_fwd[i])
        for s in range(4):
            start = (i % 2) * HALF + s * 256
            whole(i)[rows_at(member, TOK), start : start + 256] = compacted[
                s * TOK : (s + 1) * TOK, :
            ].astype(BF16)
        own = half_view(i, member, 0, HALF)
        remote(own, own, s_gather.at[i, 0], r_gather.at[i, 0], {"expert": near_x}).start()
        remote(own, own, s_gather.at[i, 1], r_gather.at[i, 1], {"expert": near_y}).start()

    def gather_forward(i):
        await_copy(half_view(i, mx, 0, HALF), r_gather.at[i, 0])
        view = half_view(i, mx, 0, CAP)
        remote(view, view, s_gather.at[i, 2], r_gather.at[i, 2], {"expert": near_y}).start()
        await_copy(half_view(i, my, 0, HALF), r_gather.at[i, 1])
        view = half_view(i, my, CAP, CAP)
        remote(view, view, s_gather.at[i, 3], r_gather.at[i, 3], {"expert": near_x}).start()

    def gather_far(i):
        await_copy(half_view(i, md, 0, CAP), r_gather.at[i, 2])
        await_copy(half_view(i, md, CAP, CAP), r_gather.at[i, 3])

    def gather_sent(i):
        await_copy(half_view(i, member, 0, HALF), s_gather.at[i, 0])
        await_copy(half_view(i, member, 0, HALF), s_gather.at[i, 1])
        await_copy(half_view(i, mx, 0, CAP), s_gather.at[i, 2])
        await_copy(half_view(i, my, CAP, CAP), s_gather.at[i, 3])

    def forward(i, block):
        at = rows_at(block, TOK)
        half = slice(i * HALF, (i + 1) * HALF)
        product = dot(rows_all[at, half], gu_full[half, :])
        pre_all[at, :] = product if i == 0 else pre_all[at, :] + product

    def upstream(i, block):
        at = rows_at(block, TOK)
        grad = grads_all[at, i * HALF : (i + 1) * HALF]
        gated_all[at, i * HALF : (i + 1) * HALF] = (gate_col[at, :] * grad.astype(F32)).astype(BF16)
        product = dot_last(grad, down_full[i])
        ups_all[at, :] = product if i == 0 else ups_all[at, :] + product

    def backward(block):
        at = rows_at(block, TOK)
        ups, pre, up = ups_all[at, :], pre_all[at, :HIDDEN], pre_all[at, HIDDEN:]
        sigmoid = jax.nn.sigmoid(pre)
        swish = pre * sigmoid
        activation = (swish * up).astype(BF16)
        part_col[at, :] = jnp.sum(activation.astype(F32) * ups, axis=1, keepdims=True)
        scaled = gate_col[at, :] * ups
        act_all[at, :] = activation
        gg_all[at, :HIDDEN] = (scaled * up * sigmoid * (1.0 + pre * (1.0 - sigmoid))).astype(BF16)
        gg_all[at, HIDDEN:] = (scaled * swish).astype(BF16)

    def input_part(block, c):
        return dot_last(gg_all[rows_at(block, TOK), :], gu_full[c * PIECE : (c + 1) * PIECE, :])

    roles = ((mx, near_x), (my, near_y), (md, far))

    def part_copy(role, c):
        return remote(
            part_send.at[role, c],
            part_recv.at[role, c],
            s_part.at[role, c],
            r_part.at[role, c],
            {"expert": roles[role][1]},
        )

    def send_part(role, c):
        part_send[role, c] = input_part(roles[role][0], c).astype(BF16)
        part_copy(role, c).start()

    gather_own(0)
    make_tables()
    gather_forward(0)
    for i, (source, target) in enumerate(weight_views):
        await_copy(target, s_own.at[i])
    for i, view in enumerate(
        (
            gu_full.at[rows_at(1 - dp, HALF), gate_cols],
            gu_full.at[rows_at(1 - dp, HALF), up_cols],
            down_full.at[1 - dp],
        )
    ):
        await_copy(view, r_w.at[i])
    gather_own(1)
    for block in (member, mx, my):
        forward(0, block)
    make_from_token()
    gather_far(0)
    gather_forward(1)
    gather_own(2)
    forward(0, md)
    for block in (member, mx, my):
        forward(1, block)
    upstream(0, member)
    gather_far(1)
    gather_forward(2)
    gather_own(3)
    forward(1, md)
    upstream(0, mx)
    upstream(0, my)
    upstream(1, member)
    backward(member)
    for c in range(PIECES):
        part_own[:, c * PIECE : (c + 1) * PIECE] = input_part(member, c)
    gather_far(2)
    upstream(0, md)
    gather_forward(3)
    for role in range(2):
        upstream(1, roles[role][0])
        backward(roles[role][0])
        send_part(role, 0)
    gather_far(3)
    upstream(1, md)
    backward(md)
    send_part(2, 0)
    for c in range(1, PIECES):
        for role in (2, 0, 1):
            send_part(role, c)

    for b in range(4):
        act_t[:, b * TOK : (b + 1) * TOK] = jnp.transpose(
            act_all[b * TOK : (b + 1) * TOK, :].astype(F32)
        ).astype(BF16)

    def weight_terms(half, gu_to, down_to):
        def step(i, carry):
            columns = pl.ds(pl.multiple_of(half * HALF + i * 256, 256), 256)
            gu_to[rows_at(i, 256), :] = dot_first(rows_all[:, columns], gg_all[...]).astype(BF16)
            down_to[:, rows_at(i, 256)] = dot(act_t[...], gated_all[:, columns]).astype(BF16)
            return carry

        lax.fori_loop(0, 4, step, 0)

    weight_terms(1 - dp, gu_send, down_send)
    term_copies = [
        remote(gu_send, gu_other, s_term.at[0], r_term.at[0], partner),
        remote(down_send, down_other, s_term.at[1], r_term.at[1], partner),
    ]
    for copy in term_copies:
        copy.start()

    def give_back(c):
        for role in range(3):
            await_copy(part_recv.at[role, c], r_part.at[role, c])
        summed[...] = (
            (part_own[:, c * PIECE : (c + 1) * PIECE] + part_recv[0, c].astype(F32))
            + (part_recv[1, c].astype(F32) + part_recv[2, c].astype(F32))
        ).astype(BF16)
        spread_rows(place_of, summed, 0, PIECE, send_back.at[c])
        exchange(send_back.at[c], recv_back.at[c], s_back.at[c], r_back.at[c], True)

    def last_copy(c):
        view = pl.ds(c * PIECE, PIECE)
        return remote(
            combined.at[:, view],
            arrived.at[:, view],
            s_fin.at[c],
            r_fin.at[c],
            {"section": 0, "expert": mirror},
        )

    def combine(c):
        drain(recv_back.at[c], r_back.at[c])
        sums = dot(from_token[...], recv_back[c]).astype(BF16)
        part = PIECE // 4
        for s in range(4):
            start = c * PIECE + s * part
            combined[:, start : start + part] = sums[s * TOK : (s + 1) * TOK, :]

        @pl.when(section == 1)
        def _():
            last_copy(c).start()

    give_back(0)

    part_row = jnp.sum(place_mat[...] * part_col[...], axis=0, keepdims=True)
    gsend[...] = jnp.zeros((8, TOK), F32)
    for i in range(4):
        gsend[i : i + 1, :] = part_row[:, i * TOK : (i + 1) * TOK]
    gate_copies = [
        remote(gsend, grecv.at[i], s_gate.at[i], r_gate.at[i], {"expert": to})
        for i, (_, to) in enumerate(roles)
    ]
    for copy in gate_copies:
        copy.start()

    give_back(1)
    weight_terms(dp, gu_keep, down_keep)
    out_copies = [
        pltpu.make_async_copy(gu_keep, gu_own, s_out.at[0]),
        pltpu.make_async_copy(down_keep, down_own, s_out.at[1]),
    ]
    for copy in out_copies:
        copy.start()
    combine(0)
    give_back(2)

    for copy in gate_copies:
        copy.wait_recv()
    gsum[...] = (gsend[...] + grecv[0]) + (grecv[1] + grecv[2])

    def spread_gate(i, carry):
        to = ((owner + i) % 16) * 4 + member
        remote(gsum, gall.at[rows_at(owner, 8)], s_spread, r_spread, {"expert": to}).start()
        return carry

    lax.fori_loop(1, 16, spread_gate, 0)
    gall[rows_at(owner, 8), :] = gsum[...]

    combine(1)
    give_back(3)
    combine(2)

    others = gall.at[pl.ds(0, 15 * 8)]
    await_copy(others, r_spread)
    for e in range(16):
        for i in range(4):
            gate_grad[e : e + 1, i * TOK : (i + 1) * TOK] = gall[e * 8 + i : e * 8 + i + 1, :]

    combine(3)

    for i in range(4):
        drain(send_fwd.at[i], s_fwd.at[i])
        gather_sent(i)
    for c in range(PIECES):
        drain(send_back.at[c], s_back.at[c])
        for role in range(3):
            await_copy(part_send.at[role, c], s_part.at[role, c])
    for copy in (*weight_copies, *gate_copies, *term_copies):
        copy.wait_send()
    await_copy(others, s_spread)
    for copy in term_copies:
        copy.wait_recv()
    for copy in out_copies:
        copy.wait()

    @pl.when(section == 1)
    def _():
        incoming[...] = jnp.zeros((TOK, WIDTH), BF16)
        for c in range(PIECES):
            last_copy(c).wait_send()

    @pl.when(section == 0)
    def _():
        for c in range(PIECES):
            last_copy(c).wait_recv()
            keep = slice(c * PIECE, (c + 1) * PIECE)
            incoming[:, keep] = arrived[:, keep]


def finish(
    incoming, gate_grad, gu_own, gu_other, down_own, down_other, *outs
):
    incoming_to, gate_grad_to, gate_to, up_to, down_to = outs
    incoming_to[...] = incoming[...]
    gate_grad_to[...] = gate_grad[...]
    total = (gu_own[...].astype(F32) + gu_other[...].astype(F32)) * 0.5
    gate_to[...] = total[:, :HIDDEN]
    up_to[...] = total[:, HIDDEN:]
    down_to[...] = (down_own[...].astype(F32) + down_other[...].astype(F32)) * 0.5


def on_device(
    layer_input, grad_output, selections, gate_values, gate_weight, up_weight, down_weight
):
    vmem = pl.BlockSpec(memory_space=pltpu.VMEM)
    hbm = pl.BlockSpec(memory_space=pl.ANY)
    shape = jax.ShapeDtypeStruct
    dma = pltpu.SemaphoreType.DMA

    def held(*dims):
        return pltpu.VMEM(dims, BF16)

    def held32(*dims):
        return pltpu.VMEM(dims, F32)

    part = PIECE // 4
    middle = pl.pallas_call(
        kernel,
        out_shape=(
            shape((TOK, WIDTH), BF16),
            shape((16, CAP), F32),
            shape((HALF, 2 * HIDDEN), BF16),
            shape((HALF, 2 * HIDDEN), BF16),
            shape((HIDDEN, HALF), BF16),
            shape((HIDDEN, HALF), BF16),
        ),
        in_specs=[vmem] * 4 + [hbm] * 3,
        out_specs=(vmem, vmem, hbm, hbm, hbm, hbm),
        scratch_shapes=[
            held(4, ALL, 256),
            held(4, ALL, 256),
            held(PIECES, ALL, part),
            held(PIECES, ALL, part),
            held(CAP, WIDTH),
            held(CAP, WIDTH),
            held(CAP, WIDTH),
            held(WIDTH, 2 * HIDDEN),
            held(2, HIDDEN, HALF),
            held32(CAP, 2 * HIDDEN),
            held32(CAP, HIDDEN),
            held(CAP, HIDDEN),
            held(HIDDEN, CAP),
            held(CAP, 2 * HIDDEN),
            pltpu.VMEM((16, TOK), jnp.int32),
            held(ALL, CAP),
            held(CAP, ALL),
            held(ALL, CAP),
            held(CAP, ALL),
            held32(CAP, 1),
            held32(CAP, 1),
            held32(CAP, CAP),
            held32(TOK, WIDTH),
            held(3, PIECES, TOK, PIECE),
            held(3, PIECES, TOK, PIECE),
            held(TOK, PIECE),
            held(HALF, 2 * HIDDEN),
            held(HALF, 2 * HIDDEN),
            held(HIDDEN, HALF),
            held(HIDDEN, HALF),
            held32(8, TOK),
            held32(3, 8, TOK),
            held32(8, TOK),
            held32(16 * 8, TOK),
            held(TOK, WIDTH),
            held(TOK, WIDTH),
            dma((4,)),
            dma((4,)),
            dma((PIECES,)),
            dma((PIECES,)),
            dma((3,)),
            dma((3,)),
            dma((3,)),
            dma((4, 4)),
            dma((4, 4)),
            dma((3, PIECES)),
            dma((3, PIECES)),
            dma((2,)),
            dma((2,)),
            dma((2,)),
            dma((3,)),
            dma((3,)),
            dma,
            dma,
            dma((PIECES,)),
            dma((PIECES,)),
        ],
        compiler_params=pltpu.CompilerParams(
            collective_id=0, has_side_effects=True, vmem_limit_bytes=56 * 2**20
        ),
        cost_estimate=pl.CostEstimate(
            flops=8_000_000_000, bytes_accessed=8_000_000, transcendentals=131072
        ),
    )(
        layer_input[0, 0],
        grad_output[0, 0],
        selections[0, 0],
        gate_values[0, 0],
        gate_weight[0, 0],
        up_weight[0, 0],
        down_weight[0, 0],
    )

    def blocks(*dims):
        return pl.BlockSpec(dims, lambda i: (i, 0))

    outs = pl.pallas_call(
        finish,
        grid=(2,),
        out_shape=(
            shape((TOK, WIDTH), BF16),
            shape((16, CAP), F32),
            shape((HALF, HIDDEN), F32),
            shape((HALF, HIDDEN), F32),
            shape((HIDDEN, HALF), F32),
        ),
        in_specs=[
            blocks(TOK // 2, WIDTH),
            blocks(8, CAP),
            blocks(CAP, 2 * HIDDEN),
            blocks(CAP, 2 * HIDDEN),
            blocks(TOK, HALF),
            blocks(TOK, HALF),
        ],
        out_specs=(
            blocks(TOK // 2, WIDTH),
            blocks(8, CAP),
            blocks(CAP, HIDDEN),
            blocks(CAP, HIDDEN),
            blocks(TOK, HALF),
        ),
        compiler_params=pltpu.CompilerParams(vmem_limit_bytes=60 * 2**20),
        cost_estimate=pl.CostEstimate(
            flops=1_000_000, bytes_accessed=7_500_000, transcendentals=0
        ),
    )(*middle)
    return tuple(out[None, None] for out in outs)


def solution(mesh):
    return jax.shard_map(
        on_device,
        mesh=mesh,
        in_specs=(
            P("section", "dp", "expert", None),
            P("section", "dp", "expert", None),
            P("section", "dp", None, None),
            P("section", "dp", None, None),
            P("section", "expert", "dp", None),
            P("section", "expert", "dp", None),
            P("section", "expert", None, "dp"),
        ),
        out_specs=(
            P("section", "dp", "expert", None),
            P("section", "dp", None, None),
            P("section", "expert", "dp", None),
            P("section", "expert", "dp", None),
            P("section", "expert", None, "dp"),
        ),
        check_vma=False,
    )
```

time: 159 us -> 133 us (0.84)
  Pallas kernels: 150 us -> 132 us
  local copies, waits for them, and re-layouts: 7.52 us -> 0 us
    pallas_call x1, Pallas kernels: 150 us -> 129 us  [on_device(): pl.pallas_call(kernel, out_shape=(shape((TOK, WIDTH), BF16), shape((16, C...]
    unnamed x11 -> x0, local copies, waits for them, and re-layouts: 7.52 us -> none
    pallas_call x0 -> x1, Pallas kernels: none -> 3.45 us  [on_device(): pl.pallas_call(finish, grid=(2,), out_shape=(shape((TOK, WIDTH), BF16), s...]
where the time goes in v2:
time: 133 us
  Pallas kernels  132 us (99%)
    pallas_call x1, Pallas kernels, on_device(): pl.pallas_call(kernel, out_shape=(shape((TOK, WIDTH), BF16), shape((16, C...  129 us
    pallas_call x1, Pallas kernels, on_device(): pl.pallas_call(finish, grid=(2,), out_shape=(shape((TOK, WIDTH), BF16), s...  3.45 us

profile of v2, /device:TPU:8, one launch (start us, length us, event | category | flops | bytes accessed | tf_op | source)
XLA Modules:
  0.0 132.6 jit_solution(18258471598263289659)
XLA Ops:
  0.6 128.6 %shard_map.110 = (bf16[128,2048]{1,0:T(8,128)(2,1)}, f32[16,512]{1,0:T(8,128)}, bf16[1024,512]{1,0:T(8,128)(2,1)}, bf16[1024,512]{1,0:T(8,128)(2,1)}, bf16[256,1...) custom-call(bf16[128,2048]{1,0:T(8,128)(2,1)} %bitcast.15, bf16[128,2048]{1,0:T(8,128)(2,1)} %bitcast.16, s32[16,512]{1,0:T(8,128)} %bitcast.21, ...), custom_call_target="tpu_custom_call" | custom-call | flops 8000000000 | bytes 8000000 | tf_op jit(solution)/shard_map/pallas_call | solution.py:622
  129.2 3.4 %shard_map.111 = (bf16[128,2048]{1,0:T(8,128)(2,1)}, f32[16,512]{1,0:T(8,128)}, f32[1024,256]{1,0:T(8,128)}, f32[1024,256]{1,0:T(8,128)}, f32[256,1024]{1,0:T(8,128)}) custom-call(bf16[128,2048]{1,0:T(8,128)(2,1)} %get-tuple-element.16.incoming, f32[16,512]{1,0:T(8,128)} %get-tuple-element.17.gate_grad, bf16[1024,512]{1,0:T(8,128)(2,1)} %get-tuple-element.18.gu_own, ...), custom_call_target="tpu_custom_call" | custom-call | flops 1000000 | bytes 7500000 | tf_op jit(solution)/shard_map/pallas_call | solution.py:711

commit v3 on v2

--- a/solution.py
+++ b/solution.py
@@ -19,6 +19,8 @@
 HALF = 1024
 PIECES = 4
 PIECE = WIDTH // PIECES
+SIDE = PIECE // 2
+CHUNKS = ((0, 0, 1024), (0, 1024, 1024), (1, 0, 1024), (1, 1024, 1024))
 
 
 def dot(left, right):
@@ -111,8 +113,8 @@
     gu_other,
     down_own,
     down_other,
-    send_fwd,
-    recv_fwd,
+    send_wide,
+    recv_wide,
     send_back,
     recv_back,
     rows_all,
@@ -134,8 +136,11 @@
     part_col,
     place_mat,
     part_own,
-    part_send,
-    part_recv,
+    part_relay,
+    first_send,
+    first_recv,
+    second_send,
+    second_recv,
     summed,
     gu_send,
     gu_keep,
@@ -156,8 +161,10 @@
     s_own,
     s_gather,
     r_gather,
-    s_part,
-    r_part,
+    s_first,
+    r_first,
+    s_second,
+    r_second,
     s_term,
     r_term,
     s_out,
@@ -223,6 +230,9 @@
     for copy in own_copies:
         copy.start()
 
+    send_fwd = [send_wide.at[i] for i in range(4)]
+    recv_fwd = [recv_wide.at[i] for i in range(4)]
+
     columns = jnp.transpose(sel[...].astype(F32))
     codes[...] = slot_codes(sel[...], columns, me)
 
@@ -236,7 +246,11 @@
         return carry
 
     lax.fori_loop(0, 16, make_to_slot, 0)
-    spread_rows(to_slot, rows, 0, HALF, send_fwd.at[0])
+    def fill(i):
+        array, start, width = CHUNKS[i]
+        spread_rows(to_slot, (rows, grads)[array], start, width, send_fwd[i])
+
+    fill(0)
 
     pl.semaphore_wait(barrier, RANKS + 1)
 
@@ -269,7 +283,7 @@
         await_copy(ref.at[pl.ds(0, (RANKS - 1) * MSG)], sem)
 
     def dispatch(i):
-        exchange(send_fwd.at[i], recv_fwd.at[i], s_fwd.at[i], r_fwd.at[i], False)
+        exchange(send_fwd[i], recv_fwd[i], s_fwd.at[i], r_fwd.at[i], False)
 
     dispatch(0)
     partner = {"dp": 1 - dp}
@@ -279,12 +293,8 @@
     ]
     for copy in weight_copies:
         copy.start()
-    spread_rows(to_slot, rows, HALF, HALF, send_fwd.at[1])
-    dispatch(1)
-    spread_rows(to_slot, grads, 0, HALF, send_fwd.at[2])
-    dispatch(2)
-    spread_rows(to_slot, grads, HALF, HALF, send_fwd.at[3])
-    dispatch(3)
+    for i in range(1, 4):
+        fill(i)
 
     mine = sel[pl.ds(owner, 1), :]
 
@@ -333,41 +343,53 @@
 
         lax.fori_loop(0, 8, step, 0)
 
-    def whole(i):
-        return rows_all if i < 2 else grads_all
-
-    def half_view(i, block, offset, width):
-        return whole(i).at[rows_at(block, TOK), pl.ds((i % 2) * HALF + offset, width)]
+    def view_of(i, block, offset, width):
+        array, start, _ = CHUNKS[i]
+        return (rows_all, grads_all)[array].at[rows_at(block, TOK), pl.ds(start + offset, width)]
+
+    def full_view(i, block):
+        return view_of(i, block, 0, CHUNKS[i][2])
+
+    def low_view(i, block):
+        return view_of(i, block, 0, CHUNKS[i][2] // 2)
+
+    def high_view(i, block):
+        return view_of(i, block, CHUNKS[i][2] // 2, CHUNKS[i][2] // 2)
+
+    def gather_copy(i, step, view, to):
+        return remote(view, view, s_gather.at[i, step], r_gather.at[i, step], {"expert": to})
 
     def gather_own(i):
-        drain(recv_fwd.at[i], r_fwd.at[i])
-        compacted = dot(place_from[...], recv_fwd[i])
+        drain(send_fwd[i], s_fwd.at[i])
+        if i < 3:
+            dispatch(i + 1)
+        drain(recv_fwd[i], r_fwd.at[i])
+        compacted = dot(place_from[...], recv_fwd[i][...])
+        array, start, width = CHUNKS[i]
+        part = width // 4
         for s in range(4):
-            start = (i % 2) * HALF + s * 256
-            whole(i)[rows_at(member, TOK), start : start + 256] = compacted[
-                s * TOK : (s + 1) * TOK, :
-            ].astype(BF16)
-        own = half_view(i, member, 0, HALF)
-        remote(own, own, s_gather.at[i, 0], r_gather.at[i, 0], {"expert": near_x}).start()
-        remote(own, own, s_gather.at[i, 1], r_gather.at[i, 1], {"expert": near_y}).start()
+            (rows_all, grads_all)[array][
+                rows_at(member, TOK), start + s * part : start + (s + 1) * part
+            ] = compacted[s * TOK : (s + 1) * TOK, :].astype(BF16)
+        own = full_view(i, member)
+        gather_copy(i, 0, own, near_x).start()
+        gather_copy(i, 1, own, near_y).start()
 
     def gather_forward(i):
-        await_copy(half_view(i, mx, 0, HALF), r_gather.at[i, 0])
-        view = half_view(i, mx, 0, CAP)
-        remote(view, view, s_gather.at[i, 2], r_gather.at[i, 2], {"expert": near_y}).start()
-        await_copy(half_view(i, my, 0, HALF), r_gather.at[i, 1])
-        view = half_view(i, my, CAP, CAP)
-        remote(view, view, s_gather.at[i, 3], r_gather.at[i, 3], {"expert": near_x}).start()
+        await_copy(full_view(i, mx), r_gather.at[i, 0])
+        gather_copy(i, 2, low_view(i, mx), near_y).start()
+        await_copy(full_view(i, my), r_gather.at[i, 1])
+        gather_copy(i, 3, high_view(i, my), near_x).start()
 
     def gather_far(i):
-        await_copy(half_view(i, md, 0, CAP), r_gather.at[i, 2])
-        await_copy(half_view(i, md, CAP, CAP), r_gather.at[i, 3])
+        await_copy(low_view(i, md), r_gather.at[i, 2])
+        await_copy(high_view(i, md), r_gather.at[i, 3])
 
     def gather_sent(i):
-        await_copy(half_view(i, member, 0, HALF), s_gather.at[i, 0])
-        await_copy(half_view(i, member, 0, HALF), s_gather.at[i, 1])
-        await_copy(half_view(i, mx, 0, CAP), s_gather.at[i, 2])
-        await_copy(half_view(i, my, CAP, CAP), s_gather.at[i, 3])
+        await_copy(full_view(i, member), s_gather.at[i, 0])
+        await_copy(full_view(i, member), s_gather.at[i, 1])
+        await_copy(low_view(i, mx), s_gather.at[i, 2])
+        await_copy(high_view(i, my), s_gather.at[i, 3])
 
     def forward(i, block):
         at = rows_at(block, TOK)
@@ -377,10 +399,13 @@
 
     def upstream(i, block):
         at = rows_at(block, TOK)
-        grad = grads_all[at, i * HALF : (i + 1) * HALF]
-        gated_all[at, i * HALF : (i + 1) * HALF] = (gate_col[at, :] * grad.astype(F32)).astype(BF16)
-        product = dot_last(grad, down_full[i])
-        ups_all[at, :] = product if i == 0 else ups_all[at, :] + product
+        _, start, width = CHUNKS[i]
+        columns = slice(start, start + width)
+        grad = grads_all[at, columns]
+        gated_all[at, columns] = (gate_col[at, :] * grad.astype(F32)).astype(BF16)
+        inner = start % HALF
+        product = dot_last(grad, down_full[start // HALF, :, inner : inner + width])
+        ups_all[at, :] = product if start == 0 else ups_all[at, :] + product
 
     def backward(block):
         at = rows_at(block, TOK)
@@ -397,20 +422,46 @@
     def input_part(block, c):
         return dot_last(gg_all[rows_at(block, TOK), :], gu_full[c * PIECE : (c + 1) * PIECE, :])
 
-    roles = ((mx, near_x), (my, near_y), (md, far))
-
-    def part_copy(role, c):
+    def first_copy(axis, c, slot):
         return remote(
-            part_send.at[role, c],
-            part_recv.at[role, c],
-            s_part.at[role, c],
-            r_part.at[role, c],
-            {"expert": roles[role][1]},
+            first_send.at[axis, c, slot],
+            first_recv.at[axis, c, slot],
+            s_first.at[axis, c, slot],
+            r_first.at[axis, c, slot],
+            {"expert": (near_x, near_y)[axis]},
         )
 
-    def send_part(role, c):
-        part_send[role, c] = input_part(roles[role][0], c).astype(BF16)
-        part_copy(role, c).start()
+    def second_copy(axis, c):
+        return remote(
+            second_send.at[axis, c],
+            second_recv.at[axis, c],
+            s_second.at[axis, c],
+            r_second.at[axis, c],
+            {"expert": (near_x, near_y)[axis]},
+        )
+
+    def first_near(c):
+        for axis, block in enumerate((mx, my)):
+            product = input_part(block, c)
+            sides = (product[:, :SIDE], product[:, SIDE:])
+            first_send[axis, c, 0] = sides[axis].astype(BF16)
+            part_relay[axis, c] = sides[1 - axis]
+            first_copy(axis, c, 0).start()
+
+    def first_far(c):
+        product = input_part(md, c).astype(BF16)
+        for axis in range(2):
+            first_send[axis, c, 1] = product[:, axis * SIDE : (axis + 1) * SIDE]
+            first_copy(axis, c, 1).start()
+
+    def relay(c):
+        for axis in range(2):
+            other = 1 - axis
+            await_copy(first_recv.at[axis, c, 1], r_first.at[axis, c, 1])
+            second_send[other, c] = (part_relay[other, c] + first_recv[axis, c, 1].astype(F32)).astype(
+                BF16
+            )
+            second_copy(other, c).start()
 
     gather_own(0)
     make_tables()
@@ -435,31 +486,28 @@
     forward(0, md)
     for block in (member, mx, my):
         forward(1, block)
-    upstream(0, member)
+    upstream(2, member)
     gather_far(1)
     gather_forward(2)
     gather_own(3)
     forward(1, md)
-    upstream(0, mx)
-    upstream(0, my)
-    upstream(1, member)
+    upstream(2, mx)
+    upstream(2, my)
+    upstream(3, member)
     backward(member)
     for c in range(PIECES):
         part_own[:, c * PIECE : (c + 1) * PIECE] = input_part(member, c)
     gather_far(2)
-    upstream(0, md)
+    upstream(2, md)
     gather_forward(3)
-    for role in range(2):
-        upstream(1, roles[role][0])
-        backward(roles[role][0])
-        send_part(role, 0)
+    for block in (mx, my):
+        upstream(3, block)
+        backward(block)
+    first_near(0)
     gather_far(3)
-    upstream(1, md)
+    upstream(3, md)
     backward(md)
-    send_part(2, 0)
-    for c in range(1, PIECES):
-        for role in (2, 0, 1):
-            send_part(role, c)
+    first_far(0)
 
     for b in range(4):
         act_t[:, b * TOK : (b + 1) * TOK] = jnp.transpose(
@@ -475,6 +523,8 @@
 
         lax.fori_loop(0, 4, step, 0)
 
+    first_far(1)
+    first_near(1)
     weight_terms(1 - dp, gu_send, down_send)
     term_copies = [
         remote(gu_send, gu_other, s_term.at[0], r_term.at[0], partner),
@@ -484,12 +534,15 @@
         copy.start()
 
     def give_back(c):
-        for role in range(3):
-            await_copy(part_recv.at[role, c], r_part.at[role, c])
-        summed[...] = (
-            (part_own[:, c * PIECE : (c + 1) * PIECE] + part_recv[0, c].astype(F32))
-            + (part_recv[1, c].astype(F32) + part_recv[2, c].astype(F32))
-        ).astype(BF16)
+        for axis in range(2):
+            await_copy(first_recv.at[axis, c, 0], r_first.at[axis, c, 0])
+            await_copy(second_recv.at[1 - axis, c], r_second.at[1 - axis, c])
+            start = c * PIECE + axis * SIDE
+            summed[:, axis * SIDE : (axis + 1) * SIDE] = (
+                part_own[:, start : start + SIDE]
+                + first_recv[axis, c, 0].astype(F32)
+                + second_recv[1 - axis, c].astype(F32)
+            ).astype(BF16)
         spread_rows(place_of, summed, 0, PIECE, send_back.at[c])
         exchange(send_back.at[c], recv_back.at[c], s_back.at[c], r_back.at[c], True)
 
@@ -515,7 +568,13 @@
         def _():
             last_copy(c).start()
 
+    relay(0)
+    first_far(2)
+    first_near(2)
     give_back(0)
+    relay(1)
+    first_far(3)
+    first_near(3)
 
     part_row = jnp.sum(place_mat[...] * part_col[...], axis=0, keepdims=True)
     gsend[...] = jnp.zeros((8, TOK), F32)
@@ -523,12 +582,30 @@
         gsend[i : i + 1, :] = part_row[:, i * TOK : (i + 1) * TOK]
     gate_copies = [
         remote(gsend, grecv.at[i], s_gate.at[i], r_gate.at[i], {"expert": to})
-        for i, (_, to) in enumerate(roles)
+        for i, to in enumerate((near_x, near_y, far))
     ]
     for copy in gate_copies:
         copy.start()
 
     give_back(1)
+    relay(2)
+
+    for copy in gate_copies:
+        copy.wait_recv()
+    gsum[...] = (gsend[...] + grecv[0]) + (grecv[1] + grecv[2])
+
+    def spread_gate(i, carry):
+        to = ((owner + i) % 16) * 4 + member
+        remote(gsum, gall.at[rows_at(owner, 8)], s_spread, r_spread, {"expert": to}).start()
+        return carry
+
+    lax.fori_loop(1, 16, spread_gate, 0)
+    gall[rows_at(owner, 8), :] = gsum[...]
+
+    give_back(2)
+    relay(3)
+    combine(0)
+    give_back(3)
     weight_terms(dp, gu_keep, down_keep)
     out_copies = [
         pltpu.make_async_copy(gu_keep, gu_own, s_out.at[0]),
@@ -536,23 +613,7 @@
     ]
     for copy in out_copies:
         copy.start()
-    combine(0)
-    give_back(2)
-
-    for copy in gate_copies:
-        copy.wait_recv()
-    gsum[...] = (gsend[...] + grecv[0]) + (grecv[1] + grecv[2])
-
-    def spread_gate(i, carry):
-        to = ((owner + i) % 16) * 4 + member
-        remote(gsum, gall.at[rows_at(owner, 8)], s_spread, r_spread, {"expert": to}).start()
-        return carry
-
-    lax.fori_loop(1, 16, spread_gate, 0)
-    gall[rows_at(owner, 8), :] = gsum[...]
-
     combine(1)
-    give_back(3)
     combine(2)
 
     others = gall.at[pl.ds(0, 15 * 8)]
@@ -564,12 +625,13 @@
     combine(3)
 
     for i in range(4):
-        drain(send_fwd.at[i], s_fwd.at[i])
         gather_sent(i)
     for c in range(PIECES):
         drain(send_back.at[c], s_back.at[c])
-        for role in range(3):
-            await_copy(part_send.at[role, c], s_part.at[role, c])
+        for axis in range(2):
+            for slot in range(2):
+                await_copy(first_send.at[axis, c, slot], s_first.at[axis, c, slot])
+            await_copy(second_send.at[axis, c], s_second.at[axis, c])
     for copy in (*weight_copies, *gate_copies, *term_copies):
         copy.wait_send()
     await_copy(others, s_spread)
@@ -655,8 +717,11 @@
             held32(CAP, 1),
             held32(CAP, CAP),
             held32(TOK, WIDTH),
-            held(3, PIECES, TOK, PIECE),
-            held(3, PIECES, TOK, PIECE),
+            held32(2, PIECES, TOK, SIDE),
+            held(2, PIECES, 2, TOK, SIDE),
+            held(2, PIECES, 2, TOK, SIDE),
+            held(2, PIECES, TOK, SIDE),
+            held(2, PIECES, TOK, SIDE),
             held(TOK, PIECE),
             held(HALF, 2 * HIDDEN),
             held(HALF, 2 * HIDDEN),
@@ -677,8 +742,10 @@
             dma((3,)),
             dma((4, 4)),
             dma((4, 4)),
-            dma((3, PIECES)),
-            dma((3, PIECES)),
+            dma((2, PIECES, 2)),
+            dma((2, PIECES, 2)),
+            dma((2, PIECES)),
+            dma((2, PIECES)),
             dma((2,)),
             dma((2,)),
             dma((2,)),
@@ -708,6 +775,8 @@
     def blocks(*dims):
         return pl.BlockSpec(dims, lambda i: (i, 0))
 
+    fixed = pl.BlockSpec((16, CAP), lambda i: (0, 0))
+
     outs = pl.pallas_call(
         finish,
         grid=(2,),
@@ -720,18 +789,18 @@
         ),
         in_specs=[
             blocks(TOK // 2, WIDTH),
-            blocks(8, CAP),
-            blocks(CAP, 2 * HIDDEN),
-            blocks(CAP, 2 * HIDDEN),
-            blocks(TOK, HALF),
-            blocks(TOK, HALF),
+            fixed,
+            blocks(HALF // 2, 2 * HIDDEN),
+            blocks(HALF // 2, 2 * HIDDEN),
+            blocks(HIDDEN // 2, HALF),
+            blocks(HIDDEN // 2, HALF),
         ],
         out_specs=(
             blocks(TOK // 2, WIDTH),
-            blocks(8, CAP),
-            blocks(CAP, HIDDEN),
-            blocks(CAP, HIDDEN),
-            blocks(TOK, HALF),
+            fixed,
+            blocks(HALF // 2, HIDDEN),
+            blocks(HALF // 2, HIDDEN),
+            blocks(HIDDEN // 2, HALF),
         ),
         compiler_params=pltpu.CompilerParams(vmem_limit_bytes=60 * 2**20),
         cost_estimate=pl.CostEstimate(

time: 133 us -> 129 us (0.970)
  Pallas kernels: 132 us -> 129 us
    pallas_call x1, Pallas kernels: 129 us -> 125 us  [on_device(): pl.pallas_call(kernel, out_shape=(shape((TOK, WIDTH), BF16), shape((16, C...]
where the time goes in v3:
time: 129 us
  Pallas kernels  129 us (100%)
    pallas_call x1, Pallas kernels, on_device(): pl.pallas_call(kernel, out_shape=(shape((TOK, WIDTH), BF16), shape((16, C...  125 us
    pallas_call x1, Pallas kernels, on_device(): pl.pallas_call(finish, grid=(2,), out_shape=(shape((TOK, WIDTH), BF16), s...  3.63 us

profile of v3, /device:TPU:8, one launch (start us, length us, event | category | flops | bytes accessed | tf_op | source)
XLA Modules:
  0.0 129.3 jit_solution(13299438733062572800)
XLA Ops:
  0.6 125.0 %shard_map.110 = (bf16[128,2048]{1,0:T(8,128)(2,1)}, f32[16,512]{1,0:T(8,128)}, bf16[1024,512]{1,0:T(8,128)(2,1)}, bf16[1024,512]{1,0:T(8,128)(2,1)}, bf16[256,1...) custom-call(bf16[128,2048]{1,0:T(8,128)(2,1)} %bitcast.15, bf16[128,2048]{1,0:T(8,128)(2,1)} %bitcast.16, s32[16,512]{1,0:T(8,128)} %bitcast.21, ...), custom_call_target="tpu_custom_call" | custom-call | flops 8000000000 | bytes 8000000 | tf_op jit(solution)/shard_map/pallas_call | solution.py:684
  125.7 3.6 %shard_map.111 = (bf16[128,2048]{1,0:T(8,128)(2,1)}, f32[16,512]{1,0:T(8,128)}, f32[1024,256]{1,0:T(8,128)}, f32[1024,256]{1,0:T(8,128)}, f32[256,1024]{1,0:T(8,128)}) custom-call(bf16[128,2048]{1,0:T(8,128)(2,1)} %get-tuple-element.16.incoming, f32[16,512]{1,0:T(8,128)} %get-tuple-element.17.gate_grad, bf16[1024,512]{1,0:T(8,128)(2,1)} %get-tuple-element.18.gu_own, ...), custom_call_target="tpu_custom_call" | custom-call | flops 1000000 | bytes 7500000 | tf_op jit(solution)/shard_map/pallas_call | solution.py:780

commit v4 on v3

--- a/solution.py
+++ b/solution.py
@@ -100,8 +100,8 @@
 
 
 def kernel(
-    rows,
-    grads,
+    rows_from,
+    grads_from,
     sel,
     gates,
     gate_w,
@@ -113,6 +113,8 @@
     gu_other,
     down_own,
     down_other,
+    rows,
+    grads,
     send_wide,
     recv_wide,
     send_back,
@@ -151,7 +153,8 @@
     gsum,
     gall,
     combined,
-    arrived,
+    zeros,
+    s_load,
     s_fwd,
     r_fwd,
     s_back,
@@ -203,6 +206,13 @@
     def await_copy(view, sem):
         pltpu.make_async_copy(view, view, sem).wait()
 
+    loads = [
+        pltpu.make_async_copy(rows_from, rows, s_load.at[0]),
+        pltpu.make_async_copy(grads_from, grads, s_load.at[1]),
+    ]
+    for copy in loads:
+        copy.start()
+
     barrier = pltpu.get_barrier_semaphore()
 
     def greet(i, carry):
@@ -250,6 +260,8 @@
         array, start, width = CHUNKS[i]
         spread_rows(to_slot, (rows, grads)[array], start, width, send_fwd[i])
 
+    for copy in loads:
+        copy.wait()
     fill(0)
 
     pl.semaphore_wait(barrier, RANKS + 1)
@@ -462,6 +474,13 @@
                 BF16
             )
             second_copy(other, c).start()
+
+    zeros[...] = jnp.zeros((TOK, WIDTH), BF16)
+    blank = pltpu.make_async_copy(zeros, incoming, s_load.at[2])
+
+    @pl.when(section == 1)
+    def _():
+        blank.start()
 
     gather_own(0)
     make_tables()
@@ -550,7 +569,7 @@
         view = pl.ds(c * PIECE, PIECE)
         return remote(
             combined.at[:, view],
-            arrived.at[:, view],
+            incoming.at[:, view],
             s_fin.at[c],
             r_fin.at[c],
             {"section": 0, "expert": mirror},
@@ -642,16 +661,14 @@
 
     @pl.when(section == 1)
     def _():
-        incoming[...] = jnp.zeros((TOK, WIDTH), BF16)
         for c in range(PIECES):
             last_copy(c).wait_send()
+        blank.wait()
 
     @pl.when(section == 0)
     def _():
         for c in range(PIECES):
             last_copy(c).wait_recv()
-            keep = slice(c * PIECE, (c + 1) * PIECE)
-            incoming[:, keep] = arrived[:, keep]
 
 
 def finish(
@@ -691,9 +708,11 @@
             shape((HIDDEN, HALF), BF16),
             shape((HIDDEN, HALF), BF16),
         ),
-        in_specs=[vmem] * 4 + [hbm] * 3,
-        out_specs=(vmem, vmem, hbm, hbm, hbm, hbm),
+        in_specs=[hbm] * 2 + [vmem] * 2 + [hbm] * 3,
+        out_specs=(hbm, vmem, hbm, hbm, hbm, hbm),
         scratch_shapes=[
+            held(TOK, WIDTH),
+            held(TOK, WIDTH),
             held(4, ALL, 256),
             held(4, ALL, 256),
             held(PIECES, ALL, part),
@@ -733,6 +752,7 @@
             held32(16 * 8, TOK),
             held(TOK, WIDTH),
             held(TOK, WIDTH),
+            dma((3,)),
             dma((4,)),
             dma((4,)),
             dma((PIECES,)),

time: 129 us -> 129 us (level)
  no operation moved by 1% of the time
where the time goes in v4:
time: 129 us
  Pallas kernels  128 us (99%)
    pallas_call x1, Pallas kernels, on_device(): pl.pallas_call(kernel, out_shape=(shape((TOK, WIDTH), BF16), shape((16, C...  125 us
    pallas_call x1, Pallas kernels, on_device(): pl.pallas_call(finish, grid=(2,), out_shape=(shape((TOK, WIDTH), BF16), s...  3.63 us

profile of v4, /device:TPU:8, one launch (start us, length us, event | category | flops | bytes accessed | tf_op | source)
XLA Modules:
  0.0 128.9 jit_solution(17414061252714815593)
XLA Ops:
  0.6 124.6 %shard_map.110 = (bf16[128,2048]{1,0:T(8,128)(2,1)}, f32[16,512]{1,0:T(8,128)}, bf16[1024,512]{1,0:T(8,128)(2,1)}, bf16[1024,512]{1,0:T(8,128)(2,1)}, bf16[256,1...) custom-call(bf16[128,2048]{1,0:T(8,128)(2,1)} %bitcast.15, bf16[128,2048]{1,0:T(8,128)(2,1)} %bitcast.16, s32[16,512]{1,0:T(8,128)} %bitcast.21, ...), custom_call_target="tpu_custom_call" | custom-call | flops 8000000000 | bytes 8000000 | tf_op jit(solution)/shard_map/pallas_call | solution.py:701
  125.3 3.6 %shard_map.111 = (bf16[128,2048]{1,0:T(8,128)(2,1)}, f32[16,512]{1,0:T(8,128)}, f32[1024,256]{1,0:T(8,128)}, f32[1024,256]{1,0:T(8,128)}, f32[256,1024]{1,0:T(8,128)}) custom-call(bf16[128,2048]{1,0:T(8,128)(2,1)} %get-tuple-element.16.incoming, f32[16,512]{1,0:T(8,128)} %get-tuple-element.17.gate_grad, bf16[1024,512]{1,0:T(8,128)(2,1)} %get-tuple-element.18.gu_own, ...), custom_call_target="tpu_custom_call" | custom-call | flops 1000000 | bytes 7500000 | tf_op jit(solution)/shard_map/pallas_call | solution.py:800
